TPU v7x, 256 devices: a whole 4x4x8 slice. The times are simulated.
256 devices in a mesh: ctx: 32 (over x, y, z_lo), exp: 8 (over z_hi, core).
Axes of the slice: x: 4, y: 4, z: 8 (z_hi: 4, z_lo: 2; z = z_hi * 2 + z_lo), core: 2. Of those that a mesh axis runs over, the one named last changes fastest.
Arguments:
- queries: bfloat16 [4, 8192, 2048], P(None, 'ctx', 'exp'), may hold values from -12 to 12
- rotated_key_heads: bfloat16 [4, 8192, 256], P(None, 'ctx'), may hold values from -12 to 12
- value_head_rows: bfloat16 [4, 8192, 256], P(None, 'ctx'), may hold values from -6 to 6
- out_proj: bfloat16 [2048, 2048], P('exp'), may hold values from -0.59765625 to 0.59765625
- norm_gain: float32 [2048], replicated, may hold values from 0.5 to 1.5
- expert_ids: int32 [32768, 1], P(('ctx', 'exp')), may hold values from 0 to 7; in each aligned block of 128 rows (0 to 127, 128 to 255, ...) at most 32 rows name the same one
- gate_weights: float32 [32768, 1], P(('ctx', 'exp')), may hold values from 0.25 to 1
- expert_gate: bfloat16 [8, 2048, 768], P('exp'), may hold values from -0.125 to 0.125
- expert_up: bfloat16 [8, 2048, 768], P('exp'), may hold values from -0.125 to 0.125
- expert_down: bfloat16 [8, 768, 2048], P('exp'), may hold values from -0.21875 to 0.21875
- grad_out: bfloat16 [32768, 2048], P(('ctx', 'exp')), may hold values from -2.5 to 2.5
Outputs:
- layer_out: bfloat16 [32768, 2048], P(('ctx', 'exp'))
- grad_hidden: bfloat16 [32768, 2048], P(('ctx', 'exp'))
- grad_gate: float32 [8, 2048, 768], P('exp', 'ctx')
- grad_up: float32 [8, 2048, 768], P('exp', 'ctx')
- grad_down: float32 [8, 768, 2048], P('exp', None, 'ctx')
Inputs may be any that keep to these rules, and one draw needn't show every extreme that they name: `expert_ids`: in the rows of one device no expert is named more than 32 times, and the experts named in one row differ from each other.
All inputs are finite; a program needn't handle non-finite values.
Results may differ from a plain program's by a relative error of at most 0.035.
Values may be sent and summed in bfloat16 or wider, within the bound.
A program may use at most 128 MiB of HBM per device.

v0:
```python
import math

import jax
import jax.numpy as jnp
from jax import lax
from jax.sharding import PartitionSpec as P

LOCAL_QUERY_HEADS = 16
LOCAL_KEY_HEADS = 2
HEAD_SIZE = 128


epsilon = 1e-06
masked_score = -1e30


def block_fold(query_heads, query_pos):
    score_scale = 1.0 / math.sqrt(query_heads.shape[4])
    last_query = jnp.max(query_pos)

    def fold_step(running, pieces, first_row):
        key_piece, value_piece = pieces
        seq_count = key_piece.shape[0]
        kv_count = query_heads.shape[2]
        sub_rows = math.gcd(key_piece.shape[1], 512)
        sub_steps = key_piece.shape[1] // sub_rows

        def visit_block(carried, sub_index):
            key_first = sub_index * sub_rows

            def compute(current):
                old_best, weight_total, weighted = current
                key_sub = lax.dynamic_slice_in_dim(
                    key_piece, sub_index * sub_rows, sub_rows, 1
                ).reshape(seq_count, sub_rows, kv_count, -1)
                value_sub = lax.dynamic_slice_in_dim(
                    value_piece, sub_index * sub_rows, sub_rows, 1
                ).reshape(seq_count, sub_rows, kv_count, -1)
                scores = (
                    jnp.einsum(
                        "sqgrd,skgd->sgrqk",
                        query_heads,
                        key_sub,
                        preferred_element_type=jnp.float32,
                    )
                    * score_scale
                )
                allowed = (key_first + jnp.arange(sub_rows))[None, :] <= query_pos[:, None]
                scores = jnp.where(allowed, scores, masked_score)
                new_best = jnp.maximum(old_best, jnp.max(scores, axis=-1))
                weights = jnp.where(allowed, jnp.exp(scores - new_best[..., None]), 0.0)
                factor = jnp.exp(old_best - new_best)
                new_total = weight_total * factor + jnp.sum(weights, axis=-1)
                blended = jnp.einsum(
                    "sgrqk,skgd->sgrqd",
                    weights.astype(jnp.bfloat16),
                    value_sub,
                    preferred_element_type=jnp.float32,
                )
                return (new_best, new_total, weighted * factor[..., None] + blended)

            def unchanged(current):
                return current

            return (lax.cond(key_first <= last_query, compute, unchanged, carried), None)

        running, _ = lax.scan(visit_block, running, jnp.arange(sub_steps))
        return running

    return fold_step


def grouped_fold(query_heads, pos_groups, running, pieces, first_row):
    folders = [block_fold(query_heads, pos_groups[0])]
    return tuple(
        (folder(state_one, pieces, first_row) for folder, state_one in zip(folders, running))
    )


def start_state(seq_count, kv_count, repeats, block_len, head_dim):
    best_start = jnp.full((seq_count, kv_count, repeats, block_len), masked_score, jnp.float32)
    total_start = jnp.zeros((seq_count, kv_count, repeats, block_len), jnp.float32)
    weighted_start = jnp.zeros((seq_count, kv_count, repeats, block_len, head_dim), jnp.float32)
    return (best_start, total_start, weighted_start)


def grouped_start(seq_count, kv_count, repeats, block_len, group_count):
    return tuple(
        (
            start_state(seq_count, kv_count, repeats, block_len // group_count, HEAD_SIZE)
            for index in range(group_count)
        )
    )


def finish_heads(running):
    best_score, weight_total, weighted = running
    scaled = weighted / weight_total[..., None]
    seq_count, kv_count, repeats, block_len, head_dim = scaled.shape
    return (
        scaled.transpose(0, 3, 1, 2, 4)
        .reshape(seq_count, block_len, kv_count * repeats * head_dim)
        .astype(jnp.bfloat16)
    )


def grouped_finish(running):
    return jnp.concatenate([finish_heads(state_one) for state_one in running], axis=1)


def own_heads(
    queries,
    rotated_key_heads,
    value_head_rows,
    owner_index,
    pos_groups,
    heads_dev,
    query_group_width,
):
    seq_count, block_len, _ = queries.shape
    kv_count = max(1, heads_dev // query_group_width)
    repeats = heads_dev // kv_count
    kv_first = owner_index * heads_dev // query_group_width
    key_mine = lax.dynamic_slice_in_dim(
        rotated_key_heads, kv_first * HEAD_SIZE, kv_count * HEAD_SIZE, 2
    )
    value_mine = lax.dynamic_slice_in_dim(
        value_head_rows, kv_first * HEAD_SIZE, kv_count * HEAD_SIZE, 2
    )
    query_heads = queries.reshape(seq_count, block_len, kv_count, repeats, HEAD_SIZE)
    running = grouped_fold(
        query_heads,
        pos_groups,
        grouped_start(seq_count, kv_count, repeats, block_len, len(pos_groups)),
        (
            lax.all_gather(key_mine, "ctx", axis=1, tiled=True),
            lax.all_gather(value_mine, "ctx", axis=1, tiled=True),
        ),
        jnp.int32(0),
    )
    return grouped_finish(running)


def on_device(
    queries,
    rotated_key_heads,
    value_head_rows,
    out_proj,
    norm_gain,
    expert_ids,
    gate_weights,
    expert_gate,
    expert_up,
    expert_down,
    grad_out,
):
    seq_count, block_len, width = queries.shape
    heads_dev = width // HEAD_SIZE
    query_group_width = LOCAL_QUERY_HEADS // LOCAL_KEY_HEADS
    exp_count = lax.axis_size("exp")
    owner_index = lax.axis_index("exp")
    ctx_index = lax.axis_index("ctx")
    pos_groups = [ctx_index * block_len + jnp.arange(block_len)]
    attended = own_heads(
        queries,
        rotated_key_heads,
        value_head_rows,
        owner_index,
        pos_groups,
        heads_dev,
        query_group_width,
    )
    flat_heads = attended.reshape(seq_count * block_len, heads_dev * HEAD_SIZE)
    hidden = lax.psum_scatter(
        jnp.dot(flat_heads, out_proj, preferred_element_type=jnp.float32).astype(jnp.bfloat16),
        "exp",
        scatter_dimension=0,
        tiled=True,
    )
    hidden_f = hidden.astype(jnp.float32)
    inv_rms = lax.rsqrt(jnp.mean(hidden_f * hidden_f, axis=1, keepdims=True) + epsilon)
    unit = hidden_f * inv_rms
    normed = (unit * norm_gain).astype(jnp.bfloat16)
    dmodel = normed.shape[1]
    tok_rows, top_count = expert_ids.shape
    local_experts = expert_gate.shape[0]
    experts = local_experts * exp_count
    capacity = min(tok_rows, 2 * tok_rows * top_count // experts)
    flat_ids = expert_ids.reshape(-1)
    chosen = (flat_ids[:, None] == jnp.arange(experts)[None, :]).astype(jnp.int32)
    earlier = jnp.cumsum(chosen, axis=0) - chosen
    target = flat_ids * capacity + jnp.sum(earlier * chosen, axis=1)
    placed = (jnp.arange(experts * capacity)[:, None] == target[None, :]).reshape(
        experts * capacity, tok_rows, top_count
    )
    selector = jnp.any(placed, axis=2).astype(jnp.bfloat16)
    weighting = jnp.sum(jnp.where(placed, gate_weights[None, :, :], 0.0), axis=2)
    send_rows = jnp.dot(selector, normed, preferred_element_type=jnp.float32).astype(jnp.bfloat16)
    send_grads = jnp.dot(
        weighting, grad_out.astype(jnp.float32), precision=lax.Precision.HIGHEST
    ).astype(jnp.bfloat16)
    recv_rows, recv_grads = (
        lax.all_to_all(
            send_rows.reshape(experts, capacity, dmodel),
            "exp",
            split_axis=0,
            concat_axis=0,
            tiled=True,
        ),
        lax.all_to_all(
            send_grads.reshape(experts, capacity, dmodel),
            "exp",
            split_axis=0,
            concat_axis=0,
            tiled=True,
        ),
    )
    arrived = recv_rows.reshape(exp_count, local_experts, capacity, dmodel)
    cotangent = recv_grads.reshape(exp_count, local_experts, capacity, dmodel)
    gate_act = jnp.einsum(
        "nesd,edf->nesf", arrived, expert_gate, preferred_element_type=jnp.float32
    )
    up_act = jnp.einsum("nesd,edf->nesf", arrived, expert_up, preferred_element_type=jnp.float32)
    sigma = jax.nn.sigmoid(gate_act)
    gated = gate_act * sigma
    hidden_units = (gated * up_act).astype(jnp.bfloat16)
    result = jnp.einsum(
        "nesf,efd->nesd", hidden_units, expert_down, preferred_element_type=jnp.float32
    ).astype(jnp.bfloat16)
    back_units = jnp.einsum(
        "nesd,efd->nesf", cotangent, expert_down, preferred_element_type=jnp.float32
    )
    back_gate = (back_units * up_act * sigma * (1.0 + gate_act * (1.0 - sigma))).astype(
        jnp.bfloat16
    )
    back_up = (back_units * gated).astype(jnp.bfloat16)
    back_in = (
        jnp.einsum("nesf,edf->nesd", back_gate, expert_gate, preferred_element_type=jnp.float32)
        + jnp.einsum("nesf,edf->nesd", back_up, expert_up, preferred_element_type=jnp.float32)
    ).astype(jnp.bfloat16)
    part_gate = jnp.einsum("nesd,nesf->edf", arrived, back_gate, preferred_element_type=jnp.float32)
    part_up = jnp.einsum("nesd,nesf->edf", arrived, back_up, preferred_element_type=jnp.float32)
    part_down = jnp.einsum(
        "nesf,nesd->efd", hidden_units, cotangent, preferred_element_type=jnp.float32
    )
    back_result, back_rows = (
        lax.all_to_all(
            result.reshape(experts, capacity, dmodel),
            "exp",
            split_axis=0,
            concat_axis=0,
            tiled=True,
        ),
        lax.all_to_all(
            back_in.reshape(experts, capacity, dmodel),
            "exp",
            split_axis=0,
            concat_axis=0,
            tiled=True,
        ),
    )
    expert_sum = jnp.dot(
        weighting.T,
        back_result.reshape(experts * capacity, dmodel).astype(jnp.float32),
        precision=lax.Precision.HIGHEST,
    )
    layer_out = (hidden_f + expert_sum).astype(jnp.bfloat16)
    back_normed = jnp.dot(
        selector.T,
        back_rows.reshape(experts * capacity, dmodel),
        preferred_element_type=jnp.float32,
    )
    scaled_back = back_normed * norm_gain
    grad_hidden = (
        grad_out.astype(jnp.float32)
        + inv_rms * (scaled_back - unit * jnp.mean(scaled_back * unit, axis=1, keepdims=True))
    ).astype(jnp.bfloat16)
    grad_gate, grad_up, grad_down = (
        lax.psum_scatter(
            part_gate.astype(jnp.bfloat16), "ctx", scatter_dimension=1, tiled=True
        ).astype(jnp.float32),
        lax.psum_scatter(
            part_up.astype(jnp.bfloat16), "ctx", scatter_dimension=1, tiled=True
        ).astype(jnp.float32),
        lax.psum_scatter(
            part_down.astype(jnp.bfloat16), "ctx", scatter_dimension=2, tiled=True
        ).astype(jnp.float32),
    )
    return (layer_out, grad_hidden, grad_gate, grad_up, grad_down)


def solution(mesh):
    in_specs = (
        P(None, "ctx", "exp"),
        P(None, "ctx", None),
        P(None, "ctx", None),
        P("exp", None),
        P(),
        P(("ctx", "exp"), None),
        P(("ctx", "exp"), None),
        P("exp", None, None),
        P("exp", None, None),
        P("exp", None, None),
        P(("ctx", "exp"), None),
    )
    out_specs = (
        P(("ctx", "exp"), None),
        P(("ctx", "exp"), None),
        P("exp", "ctx", None),
        P("exp", "ctx", None),
        P("exp", None, "ctx"),
    )
    return jax.shard_map(
        on_device, mesh=mesh, in_specs=in_specs, out_specs=out_specs, check_vma=False
    )
```

profile of v0, /device:TPU:1, one launch (start us, length us, event | category | flops | bytes accessed | tf_op | source)
XLA Modules:
  0.0 1219.7 jit_solution(17389568122441553650)
XLA Ops:
  7.2 1.8 constant_dynamic-slice_fusion.1
  9.2 1.7 constant_dynamic-slice_fusion
  10.9 0.6 add_reduce_fusion
  11.5 2.0 copy.24
  13.6 2.0 copy.25
  15.6 190.5 %all-gather.3.cloned.1.call-done = bf16[4,8192,128]{2,1,0:T(8,128)(2,1)} async-done(((bf16[4,256,128]{2,1,0:T(8,128)(2,1)}), bf16[4,8192,128]{2,1,0:T(8,128)(2,1)}) %all-gather.3.cloned.1.call-update) | async-done | bytes 8388624 | tf_op jit(solution)/shard_map/all_gather | solution.py:136
  206.1 191.8 %all-gather.5.cloned.1.call-done = bf16[4,8192,128]{2,1,0:T(8,128)(2,1)} async-done(((bf16[4,256,128]{2,1,0:T(8,128)(2,1)}), bf16[4,8192,128]{2,1,0:T(8,128)(2,1)}) %all-gather.5.cloned.1.call-update) | async-done | bytes 8388624 | tf_op jit(solution)/shard_map/all_gather | solution.py:137
  397.9 1.1 broadcast_in_dim.52
  399.0 37.7 %while.15 = (s32[]{:T(128)}, f32[4,1,2,256]{3,2,0,1:T(2,128)S(1)}, f32[4,1,2,256]{3,2,0,1:T(2,128)S(1)}, f32[4,1,2,256,128]{4,3,2,0,1:T(8,128)}, s32[16]{0:T(128...) while((s32[]{:T(128)}, f32[4,1,2,256]{3,2,0,1:T(2,128)S(1)}, ...), condition=%wide.region_6.7_spmd.clone, body=%wide.region_1.6_spmd.clone.sunk | while | flops 551164672 | bytes 25305496 | solution.py:67
  400.9 6.8 conditional.3
  401.7 2.1 fusion.2
  403.8 2.8 fusion.12
  406.6 1.0 fusion.4
  407.7 0.6 dynamic_slice.32
  409.6 0.6 dynamic_slice.32
  411.6 0.6 dynamic_slice.32
  413.5 0.6 dynamic_slice.32
  415.4 0.6 dynamic_slice.32
  417.4 0.6 dynamic_slice.32
  419.3 0.6 dynamic_slice.32
  421.2 0.6 dynamic_slice.32
  423.2 0.6 dynamic_slice.32
  425.1 0.6 dynamic_slice.32
  427.0 0.6 dynamic_slice.32
  429.0 0.6 dynamic_slice.32
  430.9 0.6 dynamic_slice.32
  432.8 0.6 dynamic_slice.32
  434.8 0.6 dynamic_slice.32
  436.7 1.6 fusion.77
  438.8 4.4 convolution_convert_fusion
  443.7 157.1 %reduce-scatter.7.cloned.1.call-done = bf16[128,2048]{1,0:T(8,128)(2,1)} async-done(((bf16[1024,2048]{1,0:T(8,128)(2,1)}), bf16[128,2048]{1,0:T(8,128)(2,1)}) %reduce-scatter.7.cloned.1.call-update) | async-done | bytes 524304 | tf_op jit(solution)/shard_map/reduce_scatter | solution.py:174
  600.8 1.2 fusion.70
  602.1 2.5 convolution_convert_fusion.1
  604.6 6.5 all-to-all-start
  611.1 3.0 convolution_convert_fusion.2
  614.1 18.6 %all-to-all-done = bf16[8,32,2048]{2,1,0:T(8,128)(2,1)} async-done(((bf16[8,32,2048]{2,1,0:T(8,128)(2,1)}), bf16[8,32,2048]{2,1,0:T(8,128)(2,1)}, u32[]{:S(2)}, u32[]{:S(2)}) %all-to-all-start) | async-done | bytes 1048608 | tf_op jit(solution)/shard_map/all_to_all | solution.py:203
  632.7 12.2 %all-to-all-start.2 = ((bf16[8,32,2048]{2,1,0:T(8,128)(2,1)}), bf16[8,32,2048]{2,1,0:T(8,128)(2,1)}, u32[]{:S(2)}, u32[]{:S(2)}) async-start(bf16[8,32,2048]{2,1,0:T(8,128)(2,1)} %bitcast.184), calls=%async_computation.3 | async-start | bytes 2097152 | tf_op jit(solution)/shard_map/all_to_all | solution.py:210
  644.9 4.2 fusion.55
  649.1 3.1 fusion.58
  652.2 19.1 %all-to-all-done.2 = bf16[8,32,2048]{2,1,0:T(8,128)(2,1)} async-done(((bf16[8,32,2048]{2,1,0:T(8,128)(2,1)}), bf16[8,32,2048]{2,1,0:T(8,128)(2,1)}, u32[]{:S(2)}, u32[]{:S(2)}) %all-to-all-start.2) | async-done | bytes 1048608 | tf_op jit(solution)/shard_map/all_to_all | solution.py:210
  671.3 3.7 multiply_convert_fusion.1
  675.0 0.7 copy-done.9
  675.7 4.0 fusion.41
  679.7 15.7 %copy.31 = bf16[1,768,2048]{1,0,2:T(2,128)(2,1)} copy(bf16[1,768,2048]{2,1,0:T(8,128)(2,1)} %fusion.41) | data formatting | bytes 6291456
  695.4 5.0 copy.40
  700.5 4.0 fusion.40
  704.6 3.9 fusion.39
  708.5 3.2 fusion.31
  711.7 2.1 fusion.45
  713.8 6.8 all-to-all-start.3
  720.6 3.0 fusion.48
  723.6 34.6 %all-to-all-done.3 = bf16[8,32,2048]{2,1,0:T(8,128)(2,1)} async-done(((bf16[8,32,2048]{2,1,0:T(8,128)(2,1)}), bf16[8,32,2048]{2,1,0:T(8,128)(2,1)}, u32[]{:S(2)}, u32[]{:S(2)}) %all-to-all-start.3) | async-done | bytes 1048608 | tf_op jit(solution)/shard_map/all_to_all | solution.py:254
  758.2 5.1 all-to-all-start.1
  763.3 2.7 fusion.65
  766.0 35.0 %all-to-all-done.1 = bf16[8,32,2048]{2,1,0:T(8,128)(2,1)} async-done(((bf16[8,32,2048]{2,1,0:T(8,128)(2,1)}), bf16[8,32,2048]{2,1,0:T(8,128)(2,1)}, u32[]{:S(2)}, u32[]{:S(2)}) %all-to-all-start.1) | async-done | bytes 1048608 | tf_op jit(solution)/shard_map/all_to_all | solution.py:247
  801.0 2.8 fusion.51
  803.8 2.7 fusion.69
  806.5 67.8 %reduce-scatter.13.cloned.1.call-done = bf16[64,768]{1,0:T(8,128)(2,1)} async-done(((bf16[2048,768]{1,0:T(8,128)(2,1)}), bf16[64,768]{1,0:T(8,128)(2,1)}) %reduce-scatter.13.cloned.1.call-update) | async-done | bytes 98320
  874.3 1.0 reshape_bitcast_fusion
  875.5 0.8 copy.27
  876.4 165.7 %reduce-scatter.11.cloned.1.call-done = bf16[1,64,768]{2,1,0:T(8,128)(2,1)} async-done(((bf16[1,2048,768]{2,1,0:T(8,128)(2,1)}), bf16[1,64,768]{2,1,0:T(8,128)(2,1)}) %reduce-scatter.11.cloned.1.call-update) | async-done | bytes 98320 | tf_op jit(solution)/shard_map/reduce_scatter | solution.py:282
  1042.0 1.6 convert_element_type.116
  1043.6 167.6 %reduce-scatter.9.cloned.1.call-done = bf16[1,64,768]{2,1,0:T(8,128)(2,1)} async-done(((bf16[1,2048,768]{2,1,0:T(8,128)(2,1)}), bf16[1,64,768]{2,1,0:T(8,128)(2,1)}) %reduce-scatter.9.cloned.1.call-update) | async-done | bytes 98320 | tf_op jit(solution)/shard_map/reduce_scatter | solution.py:279
  1211.2 1.6 convert_element_type.113
  (80 shorter events, 2.5 us)
Async XLA Ops:
  7.2 664.2 %copy-start = (bf16[1,768,2048]{2,1,0:T(8,128)(2,1)S(1)}, bf16[1,768,2048]{2,1,0:T(8,128)(2,1)}, u32[]{:S(2)}) copy-start(bf16[1,768,2048]{2,1,0:T(8,128)(2,1)} %param.24) | copy-start | bytes 9437188
  7.2 198.9 %all-gather.3.cloned.1.call-start = ((), (), s32[]{:S(2)}) async-start(), calls=%async_computation.8 | async-start | bytes 8650752 | tf_op jit(solution)/shard_map/all_gather | solution.py:136
  9.1 388.8 %all-gather.5.cloned.1.call-start = ((), (), s32[]{:S(2)}) async-start(), calls=%async_computation.9 | async-start | bytes 8650752 | tf_op jit(solution)/shard_map/all_gather | solution.py:137
  10.8 590.0 %reduce-scatter.7.cloned.1.call-start = ((), (), s32[]{:S(2)}) async-start(), calls=%async_computation.10 | async-start | bytes 4718592 | tf_op jit(solution)/shard_map/reduce_scatter | solution.py:174
  401.5 2.3 copy-start.1
  406.6 1.0 copy-start.2
  438.8 4.5 copy-start.6
  443.3 158.8 %copy-start.5 = (f32[2048]{0:T(1024)S(1)}, f32[2048]{0:T(1024)}, u32[]{:S(2)}) copy-start(f32[2048]{0:T(1024)} %param.19) | copy-start | bytes 24580
  443.3 167.8 %copy-start.7 = (f32[128,1]{0,1:T(1,128)S(1)}, f32[128,1]{0,1:T(1,128)}, u32[]{:S(2)}) copy-start(f32[128,1]{0,1:T(1,128)} %param.21) | copy-start | bytes 1540
  604.6 28.1 %all-to-all-start = ((bf16[8,32,2048]{2,1,0:T(8,128)(2,1)}), bf16[8,32,2048]{2,1,0:T(8,128)(2,1)}, u32[]{:S(2)}, u32[]{:S(2)}) async-start(bf16[8,32,2048]{2,1,0:T(8,128)(2,1)} %bitcast.185), calls=%async_computation.1 | async-start | bytes 2097152 | tf_op jit(solution)/shard_map/all_to_all | solution.py:203
  632.7 38.6 %all-to-all-start.2 = ((bf16[8,32,2048]{2,1,0:T(8,128)(2,1)}), bf16[8,32,2048]{2,1,0:T(8,128)(2,1)}, u32[]{:S(2)}, u32[]{:S(2)}) async-start(bf16[8,32,2048]{2,1,0:T(8,128)(2,1)} %bitcast.184), calls=%async_computation.3 | async-start | bytes 2097152 | tf_op jit(solution)/shard_map/all_to_all | solution.py:210
  644.9 229.5 %reduce-scatter.13.cloned.1.call-start = ((), (), s32[]{:S(2)}) async-start(), calls=%async_computation.13 | async-start | bytes 3244032
  644.9 4.2 copy-start.4
  675.0 0.7 copy-start.9
  700.5 341.5 %reduce-scatter.11.cloned.1.call-start = ((), (), s32[]{:S(2)}) async-start(), calls=%async_computation.12 | async-start | bytes 3244032 | tf_op jit(solution)/shard_map/reduce_scatter | solution.py:282
  704.6 506.7 %reduce-scatter.9.cloned.1.call-start = ((), (), s32[]{:S(2)}) async-start(), calls=%async_computation.11 | async-start | bytes 3244032 | tf_op jit(solution)/shard_map/reduce_scatter | solution.py:279
  708.5 3.2 copy-start.3
  713.8 44.4 %all-to-all-start.3 = ((bf16[8,32,2048]{2,1,0:T(8,128)(2,1)}), bf16[8,32,2048]{2,1,0:T(8,128)(2,1)}, u32[]{:S(2)}, u32[]{:S(2)}) async-start(bf16[8,32,2048]{2,1,0:T(8,128)(2,1)} %fusion.45), calls=%async_computation.4 | async-start | bytes 2097152 | tf_op jit(solution)/shard_map/all_to_all | solution.py:254
  720.6 80.4 %copy-start.8 = (f32[128,1]{0,1:T(1,128)S(1)}, f32[128,1]{0,1:T(1,128)}, u32[]{:S(2)}) copy-start(f32[128,1]{0,1:T(1,128)} %param.21) | copy-start | bytes 1540
  758.2 42.8 %all-to-all-start.1 = ((bf16[8,32,2048]{2,1,0:T(8,128)(2,1)}), bf16[8,32,2048]{2,1,0:T(8,128)(2,1)}, u32[]{:S(2)}, u32[]{:S(2)}) async-start(bf16[8,32,2048]{2,1,0:T(8,128)(2,1)} %fusion.48), calls=%async_computation.2 | async-start | bytes 2097152 | tf_op jit(solution)/shard_map/all_to_all | solution.py:247
Sparse Core Ops, SparseCore 0:
  9.8 196.2 all-gather.2
  207.9 189.9 all-gather.4
  443.4 157.3 reduce-scatter.6
  700.6 173.6 reduce-scatter.12
  876.9 165.0 reduce-scatter.10
  1044.4 166.7 reduce-scatter.8
where the time goes:
time: 1240 us; the launch traced here: 1220 us
  waiting for transfers between devices  1050 us (85%)
  matrix products  51.4 us (4%)
  local copies, waits for them, and re-layouts  42.2 us (3%)
  starting transfers between devices  30.8 us (2%)
  loops' own time  22.2 us (2%)
  between operations  14.3 us (1%)
    all_gather x1, waiting for transfers between devices, own_heads(): lax.all_gather(value_mine, 'ctx', axis=1, tiled=True)  192 us
    all_gather x1, waiting for transfers between devices, own_heads(): lax.all_gather(key_mine, 'ctx', axis=1, tiled=True)  191 us
    reduce_scatter x1, waiting for transfers between devices, on_device(): lax.psum_scatter(part_gate.astype(jnp.bfloat16), 'ctx', scatter_dimension...  168 us
    reduce_scatter x1, waiting for transfers between devices, on_device(): lax.psum_scatter(part_up.astype(jnp.bfloat16), 'ctx', scatter_dimension=1...  166 us
    reduce_scatter x1, waiting for transfers between devices, on_device(): lax.psum_scatter(jnp.dot(flat_heads, out_proj, preferred_element_type=jnp...  157 us
    unnamed x7, waiting for transfers between devices  67.9 us
    all_to_all x1, waiting for transfers between devices, on_device(): lax.all_to_all(result.reshape(experts, capacity, dmodel), 'exp', split_ax...  35 us
    all_to_all x1, waiting for transfers between devices, on_device(): lax.all_to_all(back_in.reshape(experts, capacity, dmodel), 'exp', split_a...  34.6 us
  transfers between devices with their start and end apart: 10, of which 10 were waited for; matrix products, arithmetic and copies ran while one was open for 4% of the time, Pallas kernels for 0%

commit v1 on v0

--- a/solution.py
+++ b/solution.py
@@ -3,8 +3,11 @@
 import jax
 import jax.numpy as jnp
 from jax import lax
+from jax.experimental import pallas as pl
+from jax.experimental.pallas import tpu as pltpu
 from jax.sharding import PartitionSpec as P
 
+MESH = pl.DeviceIdType.MESH
 LOCAL_QUERY_HEADS = 16
 LOCAL_KEY_HEADS = 2
 HEAD_SIZE = 128
@@ -141,6 +144,301 @@
     return grouped_finish(running)
 
 
+F = 768
+DM = 2048
+CAP = 32
+HALF = 1152
+
+
+def mesh_place():
+    ctx = lax.axis_index("ctx")
+    e = lax.axis_index("exp")
+    x = ctx // 8
+    y = lax.rem(ctx // 2, 4)
+    z = lax.rem(ctx, 2)
+    return ctx, e, x, y, z
+
+
+def ctx_of(x, y, z):
+    return x * 8 + y * 2 + z
+
+
+def wrap4(i):
+    return lax.rem(i + 4, 4)
+
+
+def greet(partners):
+    barrier = pltpu.get_barrier_semaphore()
+    for place in partners:
+        pl.semaphore_signal(barrier, inc=1, device_id=place, device_id_type=MESH)
+    pl.semaphore_wait(barrier, len(partners))
+
+
+def all_partners(ctx, e, x, y, z):
+    found = [{"exp": lax.rem(e + d, 8)} for d in range(1, 8)]
+    found += [{"ctx": ctx_of(wrap4(x + d), y, z)} for d in (1, -1)]
+    found += [{"ctx": ctx_of(x, wrap4(y + d), z)} for d in (1, -1)]
+    found += [{"ctx": ctx_of(x, y, 1 - z)}]
+    return found
+
+
+def remote(src, dst, send, recv, place):
+    return pltpu.make_async_remote_copy(
+        src_ref=src, dst_ref=dst, send_sem=send, recv_sem=recv,
+        device_id=place, device_id_type=MESH,
+    )
+
+
+class RingSum:
+    def __init__(self, index, right, left, part, slots, send, recv, base, add):
+        self.i, self.part, self.slots, self.add = index, part, slots, add
+        i = index
+        plan = [
+            (part(wrap4(i + 2), 0), right),
+            (part(wrap4(i + 2), 1), left),
+            (part(wrap4(i + 1), 1), right),
+            (part(wrap4(i - 1), 0), left),
+            (part(wrap4(i + 1), 0), right),
+            (part(wrap4(i - 1), 1), left),
+        ]
+        self.copies = [
+            remote(src, slots.at[n], send.at[base + n], recv.at[base + n], place)
+            for n, (src, place) in enumerate(plan)
+        ]
+
+    def start(self):
+        for n in range(4):
+            self.copies[n].start()
+
+    def middle(self):
+        i = self.i
+        self.copies[0].wait_recv()
+        self.add(self.part(wrap4(i + 1), 0), [self.slots.at[0]])
+        self.copies[4].start()
+        self.copies[1].wait_recv()
+        self.add(self.part(wrap4(i - 1), 1), [self.slots.at[1]])
+        self.copies[5].start()
+
+    def finish(self):
+        i = self.i
+        self.copies[3].wait_recv()
+        self.copies[4].wait_recv()
+        self.add(self.part(i, 0), [self.slots.at[3], self.slots.at[4]])
+        self.copies[2].wait_recv()
+        self.copies[5].wait_recv()
+        self.add(self.part(i, 1), [self.slots.at[2], self.slots.at[5]])
+
+    def drain(self):
+        for copy in self.copies:
+            copy.wait_send()
+
+
+def add_rows(target, others):
+    total = target[...].astype(jnp.float32)
+    for other in others:
+        total = total + other[...].astype(jnp.float32)
+    target[...] = total.astype(jnp.bfloat16)
+
+
+def add_blocks(target, others):
+    def one(k, _):
+        a, b = k // 2, lax.rem(k, 2)
+        add_rows(target.at[a, b], [o.at[a, b] for o in others])
+        return 0
+
+    lax.fori_loop(0, 4, one, 0)
+
+
+def expert_kernel(
+    rows_in, grads_in, gate_in, up_in, down_in,
+    res_out, back_out, gg_out, gu_out, gd_out,
+    xr, cr, wg, wu, wd, act_g, act_u, act, xt, ct, grad,
+    res, back, slots1a, slots1b, slots2a, slots2b, slot3,
+    wsem, lsem, a2a_send, a2a_recv, rs_send, rs_recv,
+):
+    ctx, e, x, y, z = mesh_place()
+    f32 = jnp.float32
+    weight_copies = [
+        pltpu.make_async_copy(src, dst, wsem.at[n])
+        for n, (src, dst) in enumerate(((gate_in, wg), (up_in, wu), (down_in, wd)))
+    ]
+    for copy in weight_copies:
+        copy.start()
+    greet(all_partners(ctx, e, x, y, z))
+
+    def exchange(src, dst, first):
+        own = pltpu.make_async_copy(src.at[e], dst.at[e], lsem.at[first])
+        out = []
+        for d in range(1, 8):
+            to = lax.rem(e + d, 8)
+            out.append(remote(
+                src.at[to], dst.at[e],
+                a2a_send.at[first, d], a2a_recv.at[first, d], {"exp": to},
+            ))
+        return own, out
+
+    def begin(pair):
+        own, out = pair
+        own.start()
+        for copy in out:
+            copy.start()
+
+    def arrive(pair):
+        own, out = pair
+        own.wait()
+        for copy in out:
+            copy.wait_recv()
+
+    rows_x = exchange(rows_in, xr, 0)
+    grads_x = exchange(grads_in, cr, 1)
+    res_x = exchange(res, res_out, 2)
+    back_x = exchange(back, back_out, 3)
+    begin(rows_x)
+    begin(grads_x)
+    for copy in weight_copies:
+        copy.wait()
+    arrive(rows_x)
+
+    rows = xr[...].reshape(8 * CAP, DM)
+    for n in range(3):
+        cols = slice(n * 256, (n + 1) * 256)
+        act_g[:, cols] = jnp.dot(rows, wg[:, cols], preferred_element_type=f32)
+        act_u[:, cols] = jnp.dot(rows, wu[:, cols], preferred_element_type=f32)
+    xt[...] = rows.T
+    arrive(grads_x)
+    cot = cr[...].reshape(8 * CAP, DM)
+    ct[...] = cot.T
+    over_last = (((1,), (1,)), ((), ()))
+    for n in range(3):
+        cols = slice(n * 256, (n + 1) * 256)
+        back_units = lax.dot_general(cot, wd[cols, :], over_last, preferred_element_type=f32)
+        gate_act, up_act = act_g[:, cols], act_u[:, cols]
+        sigma = jax.nn.sigmoid(gate_act)
+        gated = gate_act * sigma
+        act[:, 1536 + n * 256:1536 + (n + 1) * 256] = (gated * up_act).astype(jnp.bfloat16)
+        act[:, cols] = (
+            back_units * up_act * sigma * (1.0 + gate_act * (1.0 - sigma))
+        ).astype(jnp.bfloat16)
+        act[:, 768 + n * 256:768 + (n + 1) * 256] = (back_units * gated).astype(jnp.bfloat16)
+
+    for n in range(8):
+        cols = slice(n * 256, (n + 1) * 256)
+        res[:, :, cols] = jnp.dot(
+            act[:, 1536:], wd[:, cols], preferred_element_type=f32
+        ).astype(jnp.bfloat16).reshape(8, CAP, 256)
+    begin(res_x)
+
+    for px in range(4):
+        for py in range(2):
+            left = xt[px * 512 + py * 256:px * 512 + (py + 1) * 256, :]
+            left_c = ct[px * 512 + py * 256:px * 512 + (py + 1) * 256, :]
+            grad[px, 2 * py:2 * py + 2, :, :, 0:1536] = jnp.dot(
+                left, act[:, :1536], preferred_element_type=f32
+            ).astype(jnp.bfloat16).reshape(2, 2, 64, 1536)
+            grad[px, 2 * py:2 * py + 2, :, :, 1536:2304] = jnp.dot(
+                left_c, act[:, 1536:], preferred_element_type=f32
+            ).astype(jnp.bfloat16).reshape(2, 2, 64, 768)
+
+    in_a, in_b = pl.ds(0, HALF), pl.ds(HALF, HALF)
+    x_right, x_left = {"ctx": ctx_of(wrap4(x + 1), y, z)}, {"ctx": ctx_of(wrap4(x - 1), y, z)}
+    y_right, y_left = {"ctx": ctx_of(x, wrap4(y + 1), z)}, {"ctx": ctx_of(x, wrap4(y - 1), z)}
+    first_a = RingSum(
+        x, x_right, x_left, lambda i, h: grad.at[i, pl.ds(2 * h, 2), :, :, in_a],
+        slots1a, rs_send, rs_recv, 0, add_blocks)
+    first_b = RingSum(
+        y, y_right, y_left, lambda i, h: grad.at[pl.ds(2 * h, 2), i, :, :, in_b],
+        slots1b, rs_send, rs_recv, 6, add_blocks)
+    second_a = RingSum(
+        y, y_right, y_left, lambda i, h: grad.at[x, i, h, :, in_a],
+        slots2a, rs_send, rs_recv, 12, add_rows)
+    second_b = RingSum(
+        x, x_right, x_left, lambda i, h: grad.at[i, y, h, :, in_b],
+        slots2b, rs_send, rs_recv, 18, add_rows)
+    first_a.start()
+    first_b.start()
+
+    for n in range(8):
+        cols = slice(n * 256, (n + 1) * 256)
+        back[:, :, cols] = (
+            lax.dot_general(act[:, 0:768], wg[cols, :], over_last, preferred_element_type=f32)
+            + lax.dot_general(act[:, 768:1536], wu[cols, :], over_last, preferred_element_type=f32)
+        ).astype(jnp.bfloat16).reshape(8, CAP, 256)
+    begin(back_x)
+
+    first_a.middle()
+    first_b.middle()
+    first_a.finish()
+    second_a.start()
+    first_b.finish()
+    second_b.start()
+    second_a.middle()
+    second_b.middle()
+    second_a.finish()
+    second_b.finish()
+    last = remote(
+        grad.at[x, y, 1 - z], slot3, rs_send.at[24], rs_recv.at[24],
+        {"ctx": ctx_of(x, y, 1 - z)},
+    )
+    last.start()
+    last.wait_recv()
+    total = grad[x, y, z].astype(f32) + slot3[...].astype(f32)
+    gg_out[...] = total[:, 0:768]
+    gu_out[...] = total[:, 768:1536]
+    gd_out[...] = total[:, 1536:2304]
+    last.wait_send()
+    for ring in (first_a, first_b, second_a, second_b):
+        ring.drain()
+    arrive(res_x)
+    arrive(back_x)
+    for pair in (rows_x, grads_x, res_x, back_x):
+        for copy in pair[1]:
+            copy.wait_send()
+
+
+def expert_call(send_rows, send_grads, gate, up, down):
+    bf, f32 = jnp.bfloat16, jnp.float32
+    anywhere = pl.BlockSpec(memory_space=pl.ANY)
+    vmem = pl.BlockSpec(memory_space=pltpu.VMEM)
+    blocks = jax.ShapeDtypeStruct((8, CAP, DM), bf)
+    shard = jax.ShapeDtypeStruct((64, F), f32)
+    return pl.pallas_call(
+        expert_kernel,
+        out_shape=(blocks, blocks, shard, shard, shard),
+        in_specs=[anywhere] * 5,
+        out_specs=(anywhere, anywhere, vmem, vmem, vmem),
+        scratch_shapes=[
+            pltpu.VMEM((8, CAP, DM), bf),
+            pltpu.VMEM((8, CAP, DM), bf),
+            pltpu.VMEM((DM, F), bf),
+            pltpu.VMEM((DM, F), bf),
+            pltpu.VMEM((F, DM), bf),
+            pltpu.VMEM((8 * CAP, F), f32),
+            pltpu.VMEM((8 * CAP, F), f32),
+            pltpu.VMEM((8 * CAP, 3 * F), bf),
+            pltpu.VMEM((DM, 8 * CAP), bf),
+            pltpu.VMEM((DM, 8 * CAP), bf),
+            pltpu.VMEM((4, 4, 2, 64, 3 * F), bf),
+            pltpu.VMEM((8, CAP, DM), bf),
+            pltpu.VMEM((8, CAP, DM), bf),
+            pltpu.VMEM((6, 2, 2, 64, HALF), bf),
+            pltpu.VMEM((6, 2, 2, 64, HALF), bf),
+            pltpu.VMEM((6, 64, HALF), bf),
+            pltpu.VMEM((6, 64, HALF), bf),
+            pltpu.VMEM((64, 3 * F), bf),
+            pltpu.SemaphoreType.DMA((3,)),
+            pltpu.SemaphoreType.DMA((4,)),
+            pltpu.SemaphoreType.DMA((4, 8)),
+            pltpu.SemaphoreType.DMA((4, 8)),
+            pltpu.SemaphoreType.DMA((25,)),
+            pltpu.SemaphoreType.DMA((25,)),
+        ],
+        compiler_params=pltpu.CompilerParams(
+            collective_id=1, has_side_effects=True, vmem_limit_bytes=56 * 1024 * 1024
+        ),
+        name="expert_layer",
+    )(send_rows, send_grads, gate, up, down)
+
+
 def on_device(
     queries,
     rotated_key_heads,
@@ -199,65 +497,12 @@
     send_grads = jnp.dot(
         weighting, grad_out.astype(jnp.float32), precision=lax.Precision.HIGHEST
     ).astype(jnp.bfloat16)
-    recv_rows, recv_grads = (
-        lax.all_to_all(
-            send_rows.reshape(experts, capacity, dmodel),
-            "exp",
-            split_axis=0,
-            concat_axis=0,
-            tiled=True,
-        ),
-        lax.all_to_all(
-            send_grads.reshape(experts, capacity, dmodel),
-            "exp",
-            split_axis=0,
-            concat_axis=0,
-            tiled=True,
-        ),
-    )
-    arrived = recv_rows.reshape(exp_count, local_experts, capacity, dmodel)
-    cotangent = recv_grads.reshape(exp_count, local_experts, capacity, dmodel)
-    gate_act = jnp.einsum(
-        "nesd,edf->nesf", arrived, expert_gate, preferred_element_type=jnp.float32
-    )
-    up_act = jnp.einsum("nesd,edf->nesf", arrived, expert_up, preferred_element_type=jnp.float32)
-    sigma = jax.nn.sigmoid(gate_act)
-    gated = gate_act * sigma
-    hidden_units = (gated * up_act).astype(jnp.bfloat16)
-    result = jnp.einsum(
-        "nesf,efd->nesd", hidden_units, expert_down, preferred_element_type=jnp.float32
-    ).astype(jnp.bfloat16)
-    back_units = jnp.einsum(
-        "nesd,efd->nesf", cotangent, expert_down, preferred_element_type=jnp.float32
-    )
-    back_gate = (back_units * up_act * sigma * (1.0 + gate_act * (1.0 - sigma))).astype(
-        jnp.bfloat16
-    )
-    back_up = (back_units * gated).astype(jnp.bfloat16)
-    back_in = (
-        jnp.einsum("nesf,edf->nesd", back_gate, expert_gate, preferred_element_type=jnp.float32)
-        + jnp.einsum("nesf,edf->nesd", back_up, expert_up, preferred_element_type=jnp.float32)
-    ).astype(jnp.bfloat16)
-    part_gate = jnp.einsum("nesd,nesf->edf", arrived, back_gate, preferred_element_type=jnp.float32)
-    part_up = jnp.einsum("nesd,nesf->edf", arrived, back_up, preferred_element_type=jnp.float32)
-    part_down = jnp.einsum(
-        "nesf,nesd->efd", hidden_units, cotangent, preferred_element_type=jnp.float32
-    )
-    back_result, back_rows = (
-        lax.all_to_all(
-            result.reshape(experts, capacity, dmodel),
-            "exp",
-            split_axis=0,
-            concat_axis=0,
-            tiled=True,
-        ),
-        lax.all_to_all(
-            back_in.reshape(experts, capacity, dmodel),
-            "exp",
-            split_axis=0,
-            concat_axis=0,
-            tiled=True,
-        ),
+    back_result, back_rows, grad_gate, grad_up, grad_down = expert_call(
+        send_rows.reshape(experts, capacity, dmodel),
+        send_grads.reshape(experts, capacity, dmodel),
+        expert_gate[0],
+        expert_up[0],
+        expert_down[0],
     )
     expert_sum = jnp.dot(
         weighting.T,
@@ -275,18 +520,7 @@
         grad_out.astype(jnp.float32)
         + inv_rms * (scaled_back - unit * jnp.mean(scaled_back * unit, axis=1, keepdims=True))
     ).astype(jnp.bfloat16)
-    grad_gate, grad_up, grad_down = (
-        lax.psum_scatter(
-            part_gate.astype(jnp.bfloat16), "ctx", scatter_dimension=1, tiled=True
-        ).astype(jnp.float32),
-        lax.psum_scatter(
-            part_up.astype(jnp.bfloat16), "ctx", scatter_dimension=1, tiled=True
-        ).astype(jnp.float32),
-        lax.psum_scatter(
-            part_down.astype(jnp.bfloat16), "ctx", scatter_dimension=2, tiled=True
-        ).astype(jnp.float32),
-    )
-    return (layer_out, grad_hidden, grad_gate, grad_up, grad_down)
+    return (layer_out, grad_hidden, grad_gate[None], grad_up[None], grad_down.T[None])
 
 
 def solution(mesh):

time: 1240 us -> 734 us (0.59); the launches traced: 1220 us -> 731 us
  waiting for transfers between devices: 1050 us -> 536 us
  Pallas kernels: 0 us -> 120 us
  matrix products: 51.4 us -> 16.7 us
  starting transfers between devices: 30.8 us -> 0.12 us
  local copies, waits for them, and re-layouts: 42.2 us -> 17.6 us
    reduce_scatter x2 -> x0, waiting for transfers between devices: 333 us -> none  [the longest x1 168 us: on_device(): lax.psum_scatter(part_gate.astype(jnp.bfloat16), 'ctx', scatter_dimension...]
    pallas_call x0 -> x1, Pallas kernels: none -> 120 us  [expert_call(): pl.pallas_call(expert_kernel, out_shape=(blocks, blocks, shard, shard, sh...]
    all_to_all x4 -> x0, waiting for transfers between devices: 107 us -> none  [the longest x1 35 us: on_device(): lax.all_to_all(result.reshape(experts, capacity, dmodel), 'exp', split_ax...]
    unnamed x7 -> x3, waiting for transfers between devices: 67.9 us -> 0.05 us
    dot_general x9 -> x0, matrix products: 31.1 us -> none  [the longest x1 4.21 us: on_device(): jnp.einsum('nesd,edf->nesf', arrived, expert_gate, preferred_element_type...]
    all_to_all x4 -> x0, starting transfers between devices: 30.6 us -> none  [the longest x1 12.2 us: on_device(): lax.all_to_all(send_grads.reshape(experts, capacity, dmodel), 'exp', spli...]
    unnamed x23, local copies, waits for them, and re-layouts: 27.6 us -> 4.14 us
  transfers between devices with their start and end apart: 10 -> 3, of which waited for: 10 -> 3; matrix products, arithmetic and copies ran while one was open for 4% -> 1% of each run, Pallas kernels for 0% -> 0%
where the time goes in v1:
time: 734 us; the launch traced here: 731 us
  waiting for transfers between devices  536 us (73%)
  Pallas kernels  120 us (16%)
  loops' own time  22.4 us (3%)
  local copies, waits for them, and re-layouts  17.6 us (2%)
  matrix products  16.7 us (2%)
  between operations  13.9 us (2%)
    all_gather x1, waiting for transfers between devices, own_heads(): lax.all_gather(key_mine, 'ctx', axis=1, tiled=True)  194 us
    all_gather x1, waiting for transfers between devices, own_heads(): lax.all_gather(value_mine, 'ctx', axis=1, tiled=True)  192 us
    reduce_scatter x1, waiting for transfers between devices, on_device(): lax.psum_scatter(jnp.dot(flat_heads, out_proj, preferred_element_type=jnp...  150 us
    pallas_call x1, Pallas kernels, expert_call(): pl.pallas_call(expert_kernel, out_shape=(blocks, blocks, shard, shard, sh...  120 us
    another operation x1, loops' own time, fold_step(): running, _ = lax.scan(visit_block, running, jnp.arange(sub_steps))  21.5 us
  transfers between devices with their start and end apart: 3, of which 3 were waited for; matrix products, arithmetic and copies ran while one was open for 1% of the time, Pallas kernels for 0%

profile of v1, /device:TPU:1, one launch (start us, length us, event | category | flops | bytes accessed | tf_op | source)
XLA Modules:
  0.0 731.4 jit_solution(3273171928376479631)
XLA Ops:
  7.2 0.0 copy-start
  7.2 0.0 all-gather.3.cloned.1.call-start
  7.2 1.8 constant_dynamic-slice_fusion.1
  9.0 0.0 all-gather.3.cloned.1.call-update
  9.0 0.0 all-gather.5.cloned.1.call-start
  9.1 1.7 constant_dynamic-slice_fusion
  10.8 0.0 all-gather.5.cloned.1.call-update
  10.8 0.0 reduce-scatter.2.cloned.1.call-start
  10.8 0.6 add_reduce_fusion
  11.5 1.2 copy.18
  12.7 0.3 copy.19
  13.0 193.7 %all-gather.3.cloned.1.call-done = bf16[4,8192,128]{2,1,0:T(8,128)(2,1)} async-done(((bf16[4,256,128]{2,1,0:T(8,128)(2,1)}), bf16[4,8192,128]{2,1,0:T(8,128)(2,1)}) %all-gather.3.cloned.1.call-update) | async-done | bytes 8388624 | tf_op jit(solution)/shard_map/all_gather | solution.py:139
  206.7 192.3 %all-gather.5.cloned.1.call-done = bf16[4,8192,128]{2,1,0:T(8,128)(2,1)} async-done(((bf16[4,256,128]{2,1,0:T(8,128)(2,1)}), bf16[4,8192,128]{2,1,0:T(8,128)(2,1)}) %all-gather.5.cloned.1.call-update) | async-done | bytes 8388624 | tf_op jit(solution)/shard_map/all_gather | solution.py:140
  399.0 0.1 broadcast_in_dim.61
  399.1 37.6 %while.15 = (s32[]{:T(128)}, f32[4,1,2,256]{3,2,0,1:T(2,128)S(1)}, f32[4,1,2,256]{3,2,0,1:T(2,128)S(1)}, f32[4,1,2,256,128]{4,3,2,0,1:T(8,128)S(1)}, s32[16]{0:T...) while((s32[]{:T(128)}, f32[4,1,2,256]{3,2,0,1:T(2,128)S(1)}, ...), condition=%wide.region_6.7_spmd.clone, body=%wide.region_1.6_spmd.clone.sunk | while | flops 551164672 | bytes 16916832 | solution.py:70
  399.1 0.6 dynamic_slice.32
  401.0 6.5 conditional.3
  401.7 0.1 broadcast_compare_fusion
  401.9 1.8 fusion.2
  403.7 2.8 fusion.12
  406.5 1.0 fusion.4
  407.6 0.6 dynamic_slice.32
  409.5 0.6 dynamic_slice.32
  411.4 0.6 dynamic_slice.32
  413.4 0.6 dynamic_slice.32
  415.3 0.6 dynamic_slice.32
  417.2 0.6 dynamic_slice.32
  419.2 0.6 dynamic_slice.32
  421.1 0.6 dynamic_slice.32
  423.0 0.6 dynamic_slice.32
  425.0 0.6 dynamic_slice.32
  426.9 0.6 dynamic_slice.32
  428.8 0.6 dynamic_slice.32
  430.8 0.6 dynamic_slice.32
  432.7 0.6 dynamic_slice.32
  434.6 0.6 dynamic_slice.32
  436.7 0.3 fusion.43
  437.1 0.5 copy.20
  437.6 0.0 copy-done
  437.7 0.0 copy-start.7
  437.7 3.2 convolution_convert_fusion
  440.9 0.0 reduce-scatter.2.cloned.1.call-update
  440.9 0.0 copy-done.7
  440.9 0.1 fusion.57
  441.0 0.2 reduce_window_sum.11
  441.2 0.2 select_reduce_fusion
  441.4 0.6 copy-done.2
  441.9 0.0 copy-done.8
  441.9 2.0 convolution_convert_fusion.2
  443.9 149.9 %reduce-scatter.2.cloned.1.call-done = bf16[128,2048]{1,0:T(8,128)(2,1)} async-done(((bf16[1024,2048]{1,0:T(8,128)(2,1)}), bf16[128,2048]{1,0:T(8,128)(2,1)}) %reduce-scatter.2.cloned.1.call-update) | async-done | bytes 524304 | tf_op jit(solution)/shard_map/reduce_scatter | solution.py:472
  593.7 1.2 fusion.37
  595.0 0.0 copy-done.6
  595.0 2.6 convolution_convert_fusion.1
  597.5 119.6 %expert_layer.1 = (bf16[8,32,2048]{2,1,0:T(8,128)(2,1)}, bf16[8,32,2048]{2,1,0:T(8,128)(2,1)}, f32[64,768]{1,0:T(8,128)}, f32[64,768]{1,0:T(8,128)}, f32[64,768]{1,0:T(8,128)}) custom-call(bf16[8,32,2048]{2,1,0:T(8,128)(2,1)} %bitcast.96, bf16[8,32,2048]{2,1,0:T(8,128)(2,1)} %bitcast.95, bf16[2048,768]{1,0:T(8,128)(2,1)} %bitcast.100, ...), custom_call_target="tpu_custom_call" | custom-call | tf_op jit(solution)/shard_map/expert_layer/pallas_call | solution.py:404
  717.2 0.0 copy-start.5
  717.2 0.0 copy-start.4
  717.2 0.0 copy-start.3
  717.2 0.0 copy-done.1
  717.2 1.7 fusion.32
  719.0 2.7 fusion.27
  721.7 1.2 fusion.36
  722.9 0.7 copy.50
  723.5 0.7 copy.51
  724.2 0.7 copy.52
  (49 shorter events, 0.3 us)
Async XLA Ops:
  7.2 430.5 %copy-start = (bf16[256,2048]{1,0:T(8,128)(2,1)S(1)}, bf16[256,2048]{1,0:T(8,128)(2,1)}, u32[]{:S(2)}) copy-start(bf16[256,2048]{1,0:T(8,128)(2,1)} %param.18) | copy-start | bytes 3145732
  7.2 199.5 %all-gather.3.cloned.1.call-start = ((), (), s32[]{:S(2)}) async-start(), calls=%async_computation.1 | async-start | bytes 8650752 | tf_op jit(solution)/shard_map/all_gather | solution.py:139
  9.0 390.0 %all-gather.5.cloned.1.call-start = ((), (), s32[]{:S(2)}) async-start(), calls=%async_computation.2 | async-start | bytes 8650752 | tf_op jit(solution)/shard_map/all_gather | solution.py:140
  10.8 583.0 %reduce-scatter.2.cloned.1.call-start = ((), (), s32[]{:S(2)}) async-start(), calls=%async_computation.3 | async-start | bytes 4718592 | tf_op jit(solution)/shard_map/reduce_scatter | solution.py:472
  437.7 3.2 copy-start.7
  440.9 1.0 copy-start.2
  440.9 1.0 copy-start.8
  440.9 154.1 %copy-start.6 = (f32[2048]{0:T(1024)S(1)}, f32[2048]{0:T(1024)}, u32[]{:S(2)}) copy-start(f32[2048]{0:T(1024)} %param.19) | copy-start | bytes 24580
  597.5 119.7 %copy-start.1 = (bf16[128,2048]{1,0:T(8,128)(2,1)S(1)}, bf16[128,2048]{1,0:T(8,128)(2,1)}, u32[]{:S(2)}) copy-start(bf16[128,2048]{1,0:T(8,128)(2,1)} %reduce-scatter.2.cloned.1.call-done) | copy-start | bytes 1572868
  717.2 5.7 copy-start.5
  717.2 6.4 copy-start.4
  717.2 7.0 copy-start.3
Sparse Core Ops, SparseCore 0:
  10.4 196.2 all-gather.2
  209.1 189.9 all-gather.4
  441.0 152.6 reduce-scatter.1

commit v2 on v1

--- a/solution.py
+++ b/solution.py
@@ -15,133 +15,6 @@
 
 epsilon = 1e-06
 masked_score = -1e30
-
-
-def block_fold(query_heads, query_pos):
-    score_scale = 1.0 / math.sqrt(query_heads.shape[4])
-    last_query = jnp.max(query_pos)
-
-    def fold_step(running, pieces, first_row):
-        key_piece, value_piece = pieces
-        seq_count = key_piece.shape[0]
-        kv_count = query_heads.shape[2]
-        sub_rows = math.gcd(key_piece.shape[1], 512)
-        sub_steps = key_piece.shape[1] // sub_rows
-
-        def visit_block(carried, sub_index):
-            key_first = sub_index * sub_rows
-
-            def compute(current):
-                old_best, weight_total, weighted = current
-                key_sub = lax.dynamic_slice_in_dim(
-                    key_piece, sub_index * sub_rows, sub_rows, 1
-                ).reshape(seq_count, sub_rows, kv_count, -1)
-                value_sub = lax.dynamic_slice_in_dim(
-                    value_piece, sub_index * sub_rows, sub_rows, 1
-                ).reshape(seq_count, sub_rows, kv_count, -1)
-                scores = (
-                    jnp.einsum(
-                        "sqgrd,skgd->sgrqk",
-                        query_heads,
-                        key_sub,
-                        preferred_element_type=jnp.float32,
-                    )
-                    * score_scale
-                )
-                allowed = (key_first + jnp.arange(sub_rows))[None, :] <= query_pos[:, None]
-                scores = jnp.where(allowed, scores, masked_score)
-                new_best = jnp.maximum(old_best, jnp.max(scores, axis=-1))
-                weights = jnp.where(allowed, jnp.exp(scores - new_best[..., None]), 0.0)
-                factor = jnp.exp(old_best - new_best)
-                new_total = weight_total * factor + jnp.sum(weights, axis=-1)
-                blended = jnp.einsum(
-                    "sgrqk,skgd->sgrqd",
-                    weights.astype(jnp.bfloat16),
-                    value_sub,
-                    preferred_element_type=jnp.float32,
-                )
-                return (new_best, new_total, weighted * factor[..., None] + blended)
-
-            def unchanged(current):
-                return current
-
-            return (lax.cond(key_first <= last_query, compute, unchanged, carried), None)
-
-        running, _ = lax.scan(visit_block, running, jnp.arange(sub_steps))
-        return running
-
-    return fold_step
-
-
-def grouped_fold(query_heads, pos_groups, running, pieces, first_row):
-    folders = [block_fold(query_heads, pos_groups[0])]
-    return tuple(
-        (folder(state_one, pieces, first_row) for folder, state_one in zip(folders, running))
-    )
-
-
-def start_state(seq_count, kv_count, repeats, block_len, head_dim):
-    best_start = jnp.full((seq_count, kv_count, repeats, block_len), masked_score, jnp.float32)
-    total_start = jnp.zeros((seq_count, kv_count, repeats, block_len), jnp.float32)
-    weighted_start = jnp.zeros((seq_count, kv_count, repeats, block_len, head_dim), jnp.float32)
-    return (best_start, total_start, weighted_start)
-
-
-def grouped_start(seq_count, kv_count, repeats, block_len, group_count):
-    return tuple(
-        (
-            start_state(seq_count, kv_count, repeats, block_len // group_count, HEAD_SIZE)
-            for index in range(group_count)
-        )
-    )
-
-
-def finish_heads(running):
-    best_score, weight_total, weighted = running
-    scaled = weighted / weight_total[..., None]
-    seq_count, kv_count, repeats, block_len, head_dim = scaled.shape
-    return (
-        scaled.transpose(0, 3, 1, 2, 4)
-        .reshape(seq_count, block_len, kv_count * repeats * head_dim)
-        .astype(jnp.bfloat16)
-    )
-
-
-def grouped_finish(running):
-    return jnp.concatenate([finish_heads(state_one) for state_one in running], axis=1)
-
-
-def own_heads(
-    queries,
-    rotated_key_heads,
-    value_head_rows,
-    owner_index,
-    pos_groups,
-    heads_dev,
-    query_group_width,
-):
-    seq_count, block_len, _ = queries.shape
-    kv_count = max(1, heads_dev // query_group_width)
-    repeats = heads_dev // kv_count
-    kv_first = owner_index * heads_dev // query_group_width
-    key_mine = lax.dynamic_slice_in_dim(
-        rotated_key_heads, kv_first * HEAD_SIZE, kv_count * HEAD_SIZE, 2
-    )
-    value_mine = lax.dynamic_slice_in_dim(
-        value_head_rows, kv_first * HEAD_SIZE, kv_count * HEAD_SIZE, 2
-    )
-    query_heads = queries.reshape(seq_count, block_len, kv_count, repeats, HEAD_SIZE)
-    running = grouped_fold(
-        query_heads,
-        pos_groups,
-        grouped_start(seq_count, kv_count, repeats, block_len, len(pos_groups)),
-        (
-            lax.all_gather(key_mine, "ctx", axis=1, tiled=True),
-            lax.all_gather(value_mine, "ctx", axis=1, tiled=True),
-        ),
-        jnp.int32(0),
-    )
-    return grouped_finish(running)
 
 
 F = 768
@@ -439,6 +312,314 @@
     )(send_rows, send_grads, gate, up, down)
 
 
+class RingGather:
+    def __init__(self, index, right, left, part, send, recv, base):
+        i = index
+        plan = [
+            (part(i, None), right),
+            (part(i, None), left),
+            (part(wrap4(i - 1), 0), right),
+            (part(wrap4(i + 1), 1), left),
+        ]
+        self.copies = [
+            remote(src, src, send.at[base + n], recv.at[base + n], place)
+            for n, (src, place) in enumerate(plan)
+        ]
+
+    def start(self):
+        self.copies[0].start()
+        self.copies[1].start()
+
+    def middle(self):
+        self.copies[0].wait_recv()
+        self.copies[2].start()
+        self.copies[1].wait_recv()
+        self.copies[3].start()
+
+    def finish(self):
+        self.copies[2].wait_recv()
+        self.copies[3].wait_recv()
+
+    def drain(self):
+        for copy in self.copies:
+            copy.wait_send()
+
+
+def attention_kernel(
+    q_in, k_in, v_in, o_in, hid_out,
+    qs, kv, w, best, tot, acc, att, part_f, part_b, got,
+    lsem, q_send, q_recv, w_send, w_recv, z_send, z_recv, g_send, g_recv, s_send, s_recv,
+):
+    ctx, e, x, y, z = mesh_place()
+    f32, bf = jnp.float32, jnp.bfloat16
+    seq, core = e // 2, lax.rem(e, 2)
+    group, slot = e // 4, lax.rem(e, 4)
+    head_cols = pl.ds(pl.multiple_of(core * HEAD_SIZE, HEAD_SIZE), HEAD_SIZE)
+    own_k = pltpu.make_async_copy(k_in.at[seq, :, head_cols], kv.at[x, y, z, 0], lsem.at[0])
+    own_v = pltpu.make_async_copy(v_in.at[seq, :, head_cols], kv.at[x, y, z, 1], lsem.at[1])
+    own_k.start()
+    own_v.start()
+    greet(all_partners(ctx, e, x, y, z))
+
+    x_right, x_left = {"ctx": ctx_of(wrap4(x + 1), y, z)}, {"ctx": ctx_of(wrap4(x - 1), y, z)}
+    y_right, y_left = {"ctx": ctx_of(x, wrap4(y + 1), z)}, {"ctx": ctx_of(x, wrap4(y - 1), z)}
+
+    def ring_x(base, part):
+        return RingGather(x, x_right, x_left, part, g_send, g_recv, base)
+
+    def ring_y(base, part):
+        return RingGather(y, y_right, y_left, part, g_send, g_recv, base)
+
+    def two(h):
+        return slice(None) if h is None else pl.ds(2 * h, 2)
+
+    kv_a1 = ring_x(0, lambda i, h: kv.at[i, y, 0] if h is None else kv.at[i, y, 0, h])
+    kv_b1 = ring_y(4, lambda i, h: kv.at[x, i, 1] if h is None else kv.at[x, i, 1, h])
+    kv_a2 = ring_y(8, lambda i, h: kv.at[two(h), i, 0])
+    kv_b2 = ring_x(12, lambda i, h: kv.at[i, two(h), 1])
+    w_a1 = ring_x(16, lambda i, h: w.at[pl.ds(0, 2), i, y] if h is None else w.at[h, i, y])
+    w_b1 = ring_y(20, lambda i, h: w.at[pl.ds(2, 2), x, i] if h is None else w.at[2 + h, x, i])
+    w_a2 = ring_y(24, lambda i, h: w.at[pl.ds(0, 2), :, i] if h is None else w.at[h, :, i])
+    w_b2 = ring_x(28, lambda i, h: w.at[pl.ds(2, 2), i] if h is None else w.at[2 + h, i])
+    z_copy = remote(
+        kv.at[x, y, z], kv.at[x, y, z], z_send, z_recv, {"ctx": ctx_of(x, y, 1 - z)}
+    )
+
+    own_k.wait()
+    own_v.wait()
+    z_copy.start()
+
+    @pl.when(z == 0)
+    def _():
+        kv_a1.start()
+
+    @pl.when(z == 1)
+    def _():
+        kv_b1.start()
+
+    piece = pl.ds(pl.multiple_of((x * 4 + y) * 16, 16), 16)
+    scatters = []
+    for d in range(4):
+        s = lax.rem(seq + d, 4)
+        to = {"exp": 2 * s + group}
+        scatters.append((
+            remote(q_in.at[s], qs.at[slot], q_send.at[d], q_recv.at[slot], to),
+            remote(o_in.at[piece, :], w.at[slot, x, y], w_send.at[d], w_recv.at[slot], to),
+        ))
+    mine = core == group
+    own_q = pltpu.make_async_copy(q_in.at[seq], qs.at[slot], q_recv.at[slot])
+    own_w = pltpu.make_async_copy(o_in.at[piece, :], w.at[slot, x, y], w_recv.at[slot])
+    for n, own in ((0, own_q), (1, own_w)):
+        @pl.when(mine)
+        def _():
+            own.start()
+
+        @pl.when(jnp.logical_not(mine))
+        def _():
+            scatters[0][n].start()
+
+        for d in range(1, 4):
+            scatters[d][n].start()
+
+    z_copy.wait_recv()
+
+    @pl.when(z == 0)
+    def _():
+        kv_b1.start()
+
+    @pl.when(z == 1)
+    def _():
+        kv_a1.start()
+
+    for j in range(4):
+        pltpu.make_async_copy(qs.at[j], qs.at[j], q_recv.at[j]).wait()
+    kv_a1.middle()
+    kv_b1.middle()
+
+    scale = math.log2(math.e) / math.sqrt(HEAD_SIZE)
+    over_last = (((1,), (1,)), ((), ()))
+
+    def head_scores(j, t, key):
+        query = qs[j, :, t * HEAD_SIZE:(t + 1) * HEAD_SIZE]
+        return lax.dot_general(query, key, over_last, preferred_element_type=f32) * scale
+
+    def own_block(j, _):
+        key, value = kv[x, y, z, 0], kv[x, y, z, 1]
+        rows_at = lax.broadcasted_iota(jnp.int32, (256, 256), 0)
+        cols_at = lax.broadcasted_iota(jnp.int32, (256, 256), 1)
+        for t in range(2):
+            scores = jnp.where(cols_at <= rows_at, head_scores(j, t, key), masked_score)
+            top = jnp.max(scores, axis=1, keepdims=True)
+            weights = jnp.exp2(scores - top)
+            best[j, t] = jnp.broadcast_to(top, (256, HEAD_SIZE))
+            tot[j, t] = weights[:, :HEAD_SIZE] + weights[:, HEAD_SIZE:]
+            acc[j, t] = jnp.dot(weights.astype(bf), value, preferred_element_type=f32)
+        return 0
+
+    def fold(bx, by, bz):
+        def heads(jj, _):
+            key, value = kv[bx, by, bz, 0], kv[bx, by, bz, 1]
+            for t4 in range(4):
+                j, t = jj * 2 + t4 // 2, t4 % 2
+                scores = head_scores(j, t, key)
+                old = best[j, t]
+                new = jnp.maximum(old, jnp.max(scores, axis=1, keepdims=True))
+                weights = jnp.exp2(scores - jnp.concatenate([new, new], axis=1))
+                factor = jnp.exp2(old - new)
+                best[j, t] = new
+                tot[j, t] = tot[j, t] * factor + weights[:, :HEAD_SIZE] + weights[:, HEAD_SIZE:]
+                acc[j, t] = acc[j, t] * factor + jnp.dot(
+                    weights.astype(bf), value, preferred_element_type=f32
+                )
+            return 0
+
+        lax.fori_loop(0, 2, heads, 0)
+
+    def visit(count, place):
+        def one(i, _):
+            bx, by, bz = place(i)
+
+            @pl.when(ctx_of(bx, by, bz) < ctx)
+            def _():
+                fold(bx, by, bz)
+
+            return 0
+
+        lax.fori_loop(0, count, one, 0)
+
+    lax.fori_loop(0, 4, own_block, 0)
+    kv_a1.finish()
+    kv_a2.start()
+    kv_b1.finish()
+    kv_b2.start()
+    for j in range(4):
+        pltpu.make_async_copy(w.at[j, x, y], w.at[j, x, y], w_recv.at[j]).wait()
+    w_a1.start()
+    w_b1.start()
+
+    def first_places(i):
+        in_a = i < 3
+        bx = jnp.where(in_a, wrap4(x + 1 + i), x)
+        by = jnp.where(in_a, y, wrap4(y + i - 2))
+        last = i == 6
+        return bx, jnp.where(last, y, by), jnp.where(in_a | last, 0, 1)
+
+    def first_place(i):
+        bx, by, bz = first_places(i)
+        return jnp.where(i == 6, x, bx), by, bz
+
+    visit(jnp.where(z == 1, 7, 6), first_place)
+    kv_a2.middle()
+    kv_b2.middle()
+    w_a1.middle()
+    w_b1.middle()
+
+    def near_place(i):
+        in_a = i < 8
+        k = lax.rem(i, 8)
+        step = 1 - 2 * lax.rem(k, 2)
+        bx = jnp.where(in_a, k // 2, wrap4(x + step))
+        by = jnp.where(in_a, wrap4(y + step), k // 2)
+        return bx, by, jnp.where(in_a, 0, 1)
+
+    visit(6, near_place)
+    w_a1.finish()
+    w_a2.start()
+    w_b1.finish()
+    w_b2.start()
+    visit(10, lambda i: near_place(i + 6))
+    kv_a2.finish()
+    kv_b2.finish()
+    w_a2.middle()
+    w_b2.middle()
+
+    def far_place(i):
+        in_a = i < 4
+        k = lax.rem(i, 4)
+        bx = jnp.where(in_a, k, wrap4(x + 2))
+        by = jnp.where(in_a, wrap4(y + 2), k)
+        return bx, by, jnp.where(in_a, 0, 1)
+
+    visit(8, far_place)
+
+    for j in range(4):
+        for t in range(2):
+            total = jnp.sum(tot[j, t], axis=1, keepdims=True)
+            h = j * 2 + t
+            att[:, :, h * HEAD_SIZE:(h + 1) * HEAD_SIZE] = (
+                (acc[j, t] / total).astype(bf).reshape(2, 128, HEAD_SIZE)
+            )
+    w_a2.finish()
+    w_b2.finish()
+
+    sibling = {"exp": e + 1 - 2 * core}
+    half = remote(part_b, got, s_send, s_recv, sibling)
+
+    def project(rows, n):
+        cols = pl.ds(pl.multiple_of(n * 256, 256), 256)
+        return cols, jnp.dot(
+            rows, w[:, :, :, :, cols].reshape(1024, 256), preferred_element_type=f32
+        )
+
+    def theirs(n, _):
+        cols, value = project(att[1 - core], n)
+        part_b[:, cols] = value.astype(bf)
+        return 0
+
+    def ours(n, _):
+        cols, value = project(att[core], n)
+        part_f[:, cols] = value
+        return 0
+
+    lax.fori_loop(0, 8, theirs, 0)
+    half.start()
+    lax.fori_loop(0, 8, ours, 0)
+    half.wait_recv()
+    hid_out[...] = (part_f[...] + got[...].astype(f32)).astype(bf)
+
+    half.wait_send()
+    z_copy.wait_send()
+    for ring in (kv_a1, kv_b1, kv_a2, kv_b2, w_a1, w_b1, w_a2, w_b2):
+        ring.drain()
+    for n in range(2):
+        @pl.when(jnp.logical_not(mine))
+        def _():
+            scatters[0][n].wait_send()
+
+        for d in range(1, 4):
+            scatters[d][n].wait_send()
+
+
+def attention_call(queries, keys, values, out_proj):
+    bf, f32 = jnp.bfloat16, jnp.float32
+    anywhere = pl.BlockSpec(memory_space=pl.ANY)
+    dma = pltpu.SemaphoreType.DMA
+    return pl.pallas_call(
+        attention_kernel,
+        out_shape=jax.ShapeDtypeStruct((128, DM), bf),
+        in_specs=[anywhere] * 4,
+        out_specs=pl.BlockSpec(memory_space=pltpu.VMEM),
+        scratch_shapes=[
+            pltpu.VMEM((4, 256, 256), bf),
+            pltpu.VMEM((4, 4, 2, 2, 256, HEAD_SIZE), bf),
+            pltpu.VMEM((4, 4, 4, 16, DM), bf),
+            pltpu.VMEM((4, 2, 256, HEAD_SIZE), f32),
+            pltpu.VMEM((4, 2, 256, HEAD_SIZE), f32),
+            pltpu.VMEM((4, 2, 256, HEAD_SIZE), f32),
+            pltpu.VMEM((2, 128, 1024), bf),
+            pltpu.VMEM((128, DM), f32),
+            pltpu.VMEM((128, DM), bf),
+            pltpu.VMEM((128, DM), bf),
+            dma((2,)), dma((4,)), dma((4,)), dma((4,)), dma((4,)),
+            dma(()), dma(()), dma((32,)), dma((32,)), dma(()), dma(()),
+        ],
+        compiler_params=pltpu.CompilerParams(
+            collective_id=2, has_side_effects=True, vmem_limit_bytes=48 * 1024 * 1024
+        ),
+        name="attention",
+    )(queries, keys, values, out_proj)
+
+
 def on_device(
     queries,
     rotated_key_heads,
@@ -452,29 +633,8 @@
     expert_down,
     grad_out,
 ):
-    seq_count, block_len, width = queries.shape
-    heads_dev = width // HEAD_SIZE
-    query_group_width = LOCAL_QUERY_HEADS // LOCAL_KEY_HEADS
     exp_count = lax.axis_size("exp")
-    owner_index = lax.axis_index("exp")
-    ctx_index = lax.axis_index("ctx")
-    pos_groups = [ctx_index * block_len + jnp.arange(block_len)]
-    attended = own_heads(
-        queries,
-        rotated_key_heads,
-        value_head_rows,
-        owner_index,
-        pos_groups,
-        heads_dev,
-        query_group_width,
-    )
-    flat_heads = attended.reshape(seq_count * block_len, heads_dev * HEAD_SIZE)
-    hidden = lax.psum_scatter(
-        jnp.dot(flat_heads, out_proj, preferred_element_type=jnp.float32).astype(jnp.bfloat16),
-        "exp",
-        scatter_dimension=0,
-        tiled=True,
-    )
+    hidden = attention_call(queries, rotated_key_heads, value_head_rows, out_proj)
     hidden_f = hidden.astype(jnp.float32)
     inv_rms = lax.rsqrt(jnp.mean(hidden_f * hidden_f, axis=1, keepdims=True) + epsilon)
     unit = hidden_f * inv_rms

time: 734 us -> 228 us (0.31)
  waiting for transfers between devices: 536 us -> 0 us
  Pallas kernels: 120 us -> 209 us
  loops' own time: 22.4 us -> 0 us
  between operations: 13.9 us -> 0.7 us
  local copies, waits for them, and re-layouts: 17.6 us -> 6.4 us
  matrix products: 16.7 us -> 7.92 us
    all_gather x2 -> x0, waiting for transfers between devices: 386 us -> none  [the longest x1 194 us: own_heads(): lax.all_gather(key_mine, 'ctx', axis=1, tiled=True)]
    reduce_scatter x1 -> x0, waiting for transfers between devices: 150 us -> none  [on_device(): lax.psum_scatter(jnp.dot(flat_heads, out_proj, preferred_element_type=jnp...]
    pallas_call x0 -> x1, Pallas kernels: none -> 81.2 us  [attention_call(): pl.pallas_call(attention_kernel, out_shape=jax.ShapeDtypeStruct((128, DM)...]
    another operation x17 -> x0, loops' own time: 22.4 us -> none  [the longest x1 21.5 us: fold_step(): running, _ = lax.scan(visit_block, running, jnp.arange(sub_steps))]
    dynamic_slice x18 -> x0, local copies, waits for them, and re-layouts: 12.8 us -> none  [the longest x16 9.39 us: fold_step(): running, _ = lax.scan(visit_block, running, jnp.arange(sub_steps))]
    pallas_call x1, Pallas kernels: 120 us -> 128 us  [expert_call(): pl.pallas_call(expert_kernel, out_shape=(blocks, blocks, shard, shard, sh...]
    dot_general x3 -> x0, matrix products: 7.78 us -> none  [the longest x1 3.2 us: on_device(): jnp.dot(flat_heads, out_proj, preferred_element_type=jnp.float32)]
  transfers between devices with their start and end apart: 3 -> 0, of which waited for: 3 -> 0; matrix products, arithmetic and copies ran while one was open for 1% -> 0% of each run, Pallas kernels for 0% -> 0%
where the time goes in v2:
time: 228 us
  Pallas kernels  209 us (92%)
  matrix products  7.92 us (3%)
  local copies, waits for them, and re-layouts  6.4 us (3%)
  other arithmetic  3.82 us (2%)
    pallas_call x1, Pallas kernels, expert_call(): pl.pallas_call(expert_kernel, out_shape=(blocks, blocks, shard, shard, sh...  128 us
    pallas_call x1, Pallas kernels, attention_call(): pl.pallas_call(attention_kernel, out_shape=jax.ShapeDtypeStruct((128, DM)...  81.2 us
    unnamed x23, local copies, waits for them, and re-layouts  6.4 us

profile of v2, /device:TPU:1, one launch (start us, length us, event | category | flops | bytes accessed | tf_op | source)
XLA Modules:
  0.0 227.9 jit_solution(8404866958830775503)
XLA Ops:
  0.6 0.0 copy-start.8
  0.6 0.0 copy-start.9
  0.7 0.7 fusion.27
  1.4 0.2 reduce_window_sum.11
  1.6 0.8 select_reduce_fusion
  2.4 0.7 multiply_add_fusion
  3.1 0.0 copy-start
  3.1 1.2 copy-done
  4.3 0.0 copy-start.1
  4.3 1.0 copy-done.1
  5.3 0.0 copy-start.2
  5.3 1.0 copy-done.2
  6.4 0.0 copy-start.3
  6.4 1.0 copy-done.3
  7.4 0.0 copy-start.4
  7.4 81.2 %attention.1 = bf16[128,2048]{1,0:T(8,128)(2,1)S(1)} custom-call(bf16[4,256,256]{2,1,0:T(8,128)(2,1)S(1)} %copy-done.1, bf16[4,256,256]{2,1,0:T(8,128)(2,1)S(1)} %copy-done.2, bf16[4,256,256]{2,1,0:T(8,128)(2,1)S(1)} %copy-done.3, bf16[256,2048]{1,0:T(8,128)(2,1)S(1)} %copy-done), custom_call_target="tpu_custom_call" | custom-call | tf_op jit(solution)/shard_map/attention/pallas_call | solution.py:597
  88.7 0.2 fusion.10
  88.9 0.0 copy-done.8
  88.9 1.5 convolution_convert_fusion
  90.4 0.0 copy-done.9
  90.4 0.0 copy-done.4
  90.4 2.0 convolution_convert_fusion.1
  92.4 127.8 %expert_layer.1 = (bf16[8,32,2048]{2,1,0:T(8,128)(2,1)}, bf16[8,32,2048]{2,1,0:T(8,128)(2,1)}, f32[64,768]{1,0:T(8,128)}, f32[64,768]{1,0:T(8,128)}, f32[64,768]{1,0:T(8,128)}) custom-call(bf16[8,32,2048]{2,1,0:T(8,128)(2,1)} %bitcast.26, bf16[8,32,2048]{2,1,0:T(8,128)(2,1)} %bitcast.27, bf16[2048,768]{1,0:T(8,128)(2,1)} %bitcast.28, ...), custom_call_target="tpu_custom_call" | custom-call | tf_op jit(solution)/shard_map/expert_layer/pallas_call | solution.py:277
  220.2 2.7 %fusion = bf16[128,2048]{1,0:T(8,128)(2,1)} fusion(bf16[256,2048]{1,0:T(8,128)(2,1)} %bitcast.32, bf16[128,2048]{1,0:T(8,128)(2,1)S(1)} %attention.1, f32[128]{0:T(128)S(1)} %bitcast.39, s32[128]{0:T(128)S(1)} %multiply_add_fusion), kind=kOutput, calls=%fused_computation.4 | convolution fusion | flops 806158336 | bytes 2098176 | tf_op jit(solution)/shard_map/dot_general | solution.py:667
  222.9 0.0 copy-start.7
  222.9 0.0 copy-start.6
  222.9 0.0 copy-start.5
  222.9 1.7 fusion.5
  224.6 1.2 fusion.9
  225.8 0.0 copy-done.7
  225.8 0.7 copy.19
  226.5 0.0 copy-done.6
  226.5 0.7 copy.20
  227.2 0.0 copy-done.5
  227.2 0.7 copy.21
  (2 shorter events, 0.0 us)
Async XLA Ops:
  0.6 88.2 %copy-start.8 = (f32[2048]{0:T(1024)S(1)}, f32[2048]{0:T(1024)}, u32[]{:S(2)}) copy-start(f32[2048]{0:T(1024)} %param.15) | copy-start | bytes 24580
  0.6 89.7 %copy-start.9 = (f32[128,1]{0,1:T(1,128)S(1)}, f32[128,1]{0,1:T(1,128)}, u32[]{:S(2)}) copy-start(f32[128,1]{0,1:T(1,128)} %param.17) | copy-start | bytes 1540
  3.1 1.2 copy-start
  4.3 1.0 copy-start.1
  5.3 1.0 copy-start.2
  6.4 1.0 copy-start.3
  7.4 83.0 %copy-start.4 = (bf16[128,2048]{1,0:T(8,128)(2,1)S(1)}, bf16[128,2048]{1,0:T(8,128)(2,1)}, u32[]{:S(2)}) copy-start(bf16[128,2048]{1,0:T(8,128)(2,1)} %param.21) | copy-start | bytes 1572868
  222.9 3.0 %copy-start.7 = (f32[64,768]{1,0:T(8,128)S(1)}, f32[64,768]{1,0:T(8,128)}, u32[]{:S(2)}) copy-start(f32[64,768]{1,0:T(8,128)} %get-tuple-element.12) | copy-start | bytes 589828
  222.9 3.6 %copy-start.6 = (f32[64,768]{1,0:T(8,128)S(1)}, f32[64,768]{1,0:T(8,128)}, u32[]{:S(2)}) copy-start(f32[64,768]{1,0:T(8,128)} %get-tuple-element.13) | copy-start | bytes 589828
  222.9 4.3 %copy-start.5 = (f32[64,768]{1,0:T(8,128)S(1)}, f32[64,768]{1,0:T(8,128)}, u32[]{:S(2)}) copy-start(f32[64,768]{1,0:T(8,128)} %get-tuple-element.14) | copy-start | bytes 589828

commit v3 on v2

v3 whole, which is shorter than its diff:
```python
import math

import jax
import jax.numpy as jnp
from jax import lax
from jax.experimental import pallas as pl
from jax.experimental.pallas import tpu as pltpu
from jax.sharding import PartitionSpec as P

MESH = pl.DeviceIdType.MESH
HEAD_SIZE = 128
F = 768
DM = 2048
CAP = 32
SLOTS = 8 * CAP
TOK = 128
CHAINS = ((0, 640), (1152, 640), (640, 512), (1792, 512))

epsilon = 1e-06
masked_score = -1e30


def mesh_place():
    ctx = lax.axis_index("ctx")
    e = lax.axis_index("exp")
    x = ctx // 8
    y = lax.rem(ctx // 2, 4)
    z = lax.rem(ctx, 2)
    return ctx, e, x, y, z


def ctx_of(x, y, z):
    return x * 8 + y * 2 + z


def wrap4(i):
    return lax.rem(i + 4, 4)


def greet(partners):
    barrier = pltpu.get_barrier_semaphore()
    for place in partners:
        pl.semaphore_signal(barrier, inc=1, device_id=place, device_id_type=MESH)
    pl.semaphore_wait(barrier, len(partners))


def all_partners(ctx, e, x, y, z):
    found = [{"exp": lax.rem(e + d, 8)} for d in range(1, 8)]
    found += [{"ctx": ctx_of(wrap4(x + d), y, z)} for d in (1, -1)]
    found += [{"ctx": ctx_of(x, wrap4(y + d), z)} for d in (1, -1)]
    found += [{"ctx": ctx_of(x, y, 1 - z)}]
    return found


def remote(src, dst, send, recv, place):
    return pltpu.make_async_remote_copy(
        src_ref=src, dst_ref=dst, send_sem=send, recv_sem=recv,
        device_id=place, device_id_type=MESH,
    )


class RingSum:
    def __init__(self, index, right, left, part, slots, send, recv, base, add):
        self.i, self.part, self.slots, self.add = index, part, slots, add
        i = index
        plan = [
            (part(wrap4(i + 2), 0), right),
            (part(wrap4(i + 2), 1), left),
            (part(wrap4(i + 1), 1), right),
            (part(wrap4(i - 1), 0), left),
            (part(wrap4(i + 1), 0), right),
            (part(wrap4(i - 1), 1), left),
        ]
        self.copies = [
            remote(src, slots.at[n], send.at[base + n], recv.at[base + n], place)
            for n, (src, place) in enumerate(plan)
        ]

    def start(self, *chosen):
        for n in chosen or range(4):
            self.copies[n].start()

    def middle(self):
        i = self.i
        self.copies[0].wait_recv()
        self.add(self.part(wrap4(i + 1), 0), [self.slots.at[0]])
        self.copies[4].start()
        self.copies[1].wait_recv()
        self.add(self.part(wrap4(i - 1), 1), [self.slots.at[1]])
        self.copies[5].start()

    def finish(self):
        i = self.i
        self.copies[3].wait_recv()
        self.copies[4].wait_recv()
        self.add(self.part(i, 0), [self.slots.at[3], self.slots.at[4]])
        self.copies[2].wait_recv()
        self.copies[5].wait_recv()
        self.add(self.part(i, 1), [self.slots.at[2], self.slots.at[5]])

    def drain(self):
        for copy in self.copies:
            copy.wait_send()


def add_rows(target, others):
    total = target[...].astype(jnp.float32)
    for other in others:
        total = total + other[...].astype(jnp.float32)
    target[...] = total.astype(jnp.bfloat16)


def add_blocks(target, others):
    def one(k, _):
        a, b = k // 2, lax.rem(k, 2)
        add_rows(target.at[a, b], [o.at[a, b] for o in others])
        return 0

    lax.fori_loop(0, 4, one, 0)


class RingGather:
    def __init__(self, index, right, left, part, send, recv, base):
        i = index
        plan = [
            (part(i, None), right),
            (part(i, None), left),
            (part(wrap4(i - 1), 0), right),
            (part(wrap4(i + 1), 1), left),
        ]
        self.copies = [
            remote(src, src, send.at[base + n], recv.at[base + n], place)
            for n, (src, place) in enumerate(plan)
        ]

    def start(self):
        self.copies[0].start()
        self.copies[1].start()

    def middle(self):
        self.copies[0].wait_recv()
        self.copies[2].start()
        self.copies[1].wait_recv()
        self.copies[3].start()

    def finish(self):
        self.copies[2].wait_recv()
        self.copies[3].wait_recv()

    def drain(self):
        for copy in self.copies:
            copy.wait_send()


def layer_kernel(
    q_in, k_in, v_in, o_in, gain_in, ids_in, weights_in, gate_in, up_in, down_in, grad_in,
    layer_out, hidden_grad_out, gg_out, gu_out, gd_out,
    qs, kv, w, best, tot, acc, att, part_f, part_b, got,
    sel, sel_t, hidden_s, rows_s, grads_s, xr, cr, wg, wu, wd,
    act_g, act_u, act_b, act, xt, ct, grad, res, back, res_r, back_r,
    slots1_wide, slots1_slim, slots2_wide, slots2_slim, slot3_wide, slot3_slim,
    lsem, q_send, q_recv, w_send, w_recv, z_send, z_recv, g_send, g_recv, s_send, s_recv,
    a2a_local, a2a_send, a2a_recv, rs_send, rs_recv,
):
    ctx, e, x, y, z = mesh_place()
    f32, bf = jnp.float32, jnp.bfloat16
    seq, core = e // 2, lax.rem(e, 2)
    group, slot = e // 4, lax.rem(e, 4)
    head_cols = pl.ds(pl.multiple_of(core * HEAD_SIZE, HEAD_SIZE), HEAD_SIZE)
    own_k = pltpu.make_async_copy(k_in.at[seq, :, head_cols], kv.at[x, y, z, 0], lsem.at[0])
    own_v = pltpu.make_async_copy(v_in.at[seq, :, head_cols], kv.at[x, y, z, 1], lsem.at[1])
    own_k.start()
    own_v.start()
    weight_copies = [
        pltpu.make_async_copy(src, dst, lsem.at[2 + n])
        for n, (src, dst) in enumerate(((gate_in, wg), (up_in, wu), (down_in, wd)))
    ]
    greet(all_partners(ctx, e, x, y, z))

    x_right, x_left = {"ctx": ctx_of(wrap4(x + 1), y, z)}, {"ctx": ctx_of(wrap4(x - 1), y, z)}
    y_right, y_left = {"ctx": ctx_of(x, wrap4(y + 1), z)}, {"ctx": ctx_of(x, wrap4(y - 1), z)}

    def ring_x(base, part):
        return RingGather(x, x_right, x_left, part, g_send, g_recv, base)

    def ring_y(base, part):
        return RingGather(y, y_right, y_left, part, g_send, g_recv, base)

    def two(h):
        return slice(None) if h is None else pl.ds(2 * h, 2)

    kv_a1 = ring_x(0, lambda i, h: kv.at[i, y, 0] if h is None else kv.at[i, y, 0, h])
    kv_b1 = ring_y(4, lambda i, h: kv.at[x, i, 1] if h is None else kv.at[x, i, 1, h])
    kv_a2 = ring_y(8, lambda i, h: kv.at[two(h), i, 0])
    kv_b2 = ring_x(12, lambda i, h: kv.at[i, two(h), 1])
    w_a1 = ring_x(16, lambda i, h: w.at[pl.ds(0, 2), i, y] if h is None else w.at[h, i, y])
    w_b1 = ring_y(20, lambda i, h: w.at[pl.ds(2, 2), x, i] if h is None else w.at[2 + h, x, i])
    w_a2 = ring_y(24, lambda i, h: w.at[pl.ds(0, 2), :, i] if h is None else w.at[h, :, i])
    w_b2 = ring_x(28, lambda i, h: w.at[pl.ds(2, 2), i] if h is None else w.at[2 + h, i])
    z_partner = {"ctx": ctx_of(x, y, 1 - z)}
    z_copy = remote(kv.at[x, y, z], kv.at[x, y, z], z_send, z_recv, z_partner)

    own_k.wait()
    own_v.wait()
    z_copy.start()

    @pl.when(z == 0)
    def _():
        kv_a1.start()

    @pl.when(z == 1)
    def _():
        kv_b1.start()

    piece = pl.ds(pl.multiple_of((x * 4 + y) * 16, 16), 16)
    scatters = []
    for d in range(4):
        to = {"exp": 2 * lax.rem(seq + d, 4) + group}
        scatters.append((
            remote(
                q_in.at[lax.rem(seq + d, 4)], qs.at[slot], q_send.at[d], q_recv.at[slot], to
            ),
            remote(o_in.at[piece, :], w.at[slot, x, y], w_send.at[d], w_recv.at[slot], to),
        ))
    mine = core == group
    own_q = pltpu.make_async_copy(q_in.at[seq], qs.at[slot], q_recv.at[slot])
    own_w = pltpu.make_async_copy(o_in.at[piece, :], w.at[slot, x, y], w_recv.at[slot])
    for n, own in ((0, own_q), (1, own_w)):
        @pl.when(mine)
        def _():
            own.start()

        @pl.when(jnp.logical_not(mine))
        def _():
            scatters[0][n].start()

        for d in range(1, 4):
            scatters[d][n].start()
    for copy in weight_copies:
        copy.start()

    z_copy.wait_recv()

    @pl.when(z == 0)
    def _():
        kv_b1.start()

    @pl.when(z == 1)
    def _():
        kv_a1.start()

    def exchange(src, dst, number):
        own = pltpu.make_async_copy(src.at[e], dst.at[e], a2a_local.at[number])
        out = []
        for d in range(1, 8):
            to = lax.rem(e + d, 8)
            out.append(remote(
                src.at[to], dst.at[e],
                a2a_send.at[number, d], a2a_recv.at[number, d], {"exp": to},
            ))
        return own, out

    def begin(pair):
        own, out = pair
        for copy in out:
            copy.start()
        own.start()

    def arrive(pair):
        own, out = pair
        own.wait()
        for copy in out:
            copy.wait_recv()

    rows_x = exchange(rows_s, xr, 0)
    grads_x = exchange(grads_s, cr, 1)
    res_x = exchange(res, res_r, 2)
    back_x = exchange(back, back_r, 3)

    ids = ids_in[...]
    lanes = lax.broadcasted_iota(jnp.int32, (TOK, TOK), 1)
    chosen = (lanes == ids).astype(f32)
    before = (lanes < lax.broadcasted_iota(jnp.int32, (TOK, TOK), 0)).astype(bf)
    earlier = jnp.dot(before, chosen.astype(bf), preferred_element_type=f32)
    place = ids.astype(f32) * CAP + jnp.sum(earlier * chosen, axis=1, keepdims=True)
    slot_at = lax.broadcasted_iota(jnp.int32, (TOK, SLOTS), 1).astype(f32)
    taken = (slot_at == place).astype(f32)
    sel_t[...] = taken.astype(bf)
    sel[...] = taken.T.astype(bf)
    gates = weights_in[...]

    def dispatch(dst, value, n):
        cols = slice(n * 256, (n + 1) * 256)
        dst[:, :, cols] = jnp.dot(
            sel[...], value, preferred_element_type=f32
        ).astype(bf).reshape(8, CAP, 256)

    for n in range(8):
        cols = slice(n * 256, (n + 1) * 256)
        dispatch(grads_s, (grad_in[:, cols].astype(f32) * gates).astype(bf), n)
    begin(grads_x)

    kv_a1.middle()
    kv_b1.middle()
    kv_a1.finish()
    kv_a2.start()
    kv_b1.finish()
    kv_b2.start()
    for j in range(4):
        pltpu.make_async_copy(qs.at[j], qs.at[j], q_recv.at[j]).wait()

    scale = math.log2(math.e) / math.sqrt(HEAD_SIZE)
    over_last = (((1,), (1,)), ((), ()))

    def head_scores(h, key):
        t = h % 2
        query = qs[h // 2, :, t * HEAD_SIZE:(t + 1) * HEAD_SIZE]
        return lax.dot_general(query, key, over_last, preferred_element_type=f32) * scale

    def with_ones(value):
        return jnp.concatenate([value, jnp.ones(value.shape, bf)], axis=1)

    key, value = kv[x, y, z, 0], with_ones(kv[x, y, z, 1])
    below = lax.broadcasted_iota(jnp.int32, (256, 256), 1) <= lax.broadcasted_iota(
        jnp.int32, (256, 256), 0
    )
    for h in range(8):
        scores = jnp.where(below, head_scores(h, key), masked_score)
        top = jnp.max(scores, axis=1, keepdims=True)
        blended = jnp.dot(jnp.exp2(scores - top).astype(bf), value, preferred_element_type=f32)
        best[h] = jnp.broadcast_to(top, (256, HEAD_SIZE))
        acc[h] = blended[:, :HEAD_SIZE]
        tot[h] = blended[:, HEAD_SIZE:]

    def fold(places):
        key = jnp.concatenate([kv[bx, by, bz, 0] for bx, by, bz in places], axis=0)
        value = with_ones(jnp.concatenate([kv[bx, by, bz, 1] for bx, by, bz in places], axis=0))
        for h in range(8):
            scores = head_scores(h, key)
            old = best[h]
            new = jnp.maximum(old, jnp.max(scores, axis=1, keepdims=True))
            weights = jnp.exp2(scores - jnp.concatenate([new] * (2 * len(places)), axis=1))
            factor = jnp.exp2(old - new)
            blended = jnp.dot(weights.astype(bf), value, preferred_element_type=f32)
            best[h] = new
            acc[h] = acc[h] * factor + blended[:, :HEAD_SIZE]
            tot[h] = tot[h] * factor + blended[:, HEAD_SIZE:]

    def four(g):
        even = lax.rem(g, 2) == 0
        k = g // 2
        off = jnp.where(k == 2, -1, jnp.where(k == 3, 2, k))
        line = jnp.where(even, wrap4(y + off), wrap4(x + off))

        def at(i):
            return jnp.where(even, i, line), jnp.where(even, line, i), jnp.where(even, 0, 1)

        whole = ctx_of(*at(3)) < ctx

        @pl.when(whole)
        def _():
            fold([at(i) for i in range(4)])

        @pl.when(jnp.logical_not(whole))
        def _():
            def one(i, _):
                bx, by, bz = at(i)

                @pl.when(ctx_of(bx, by, bz) < ctx)
                def _():
                    fold([(bx, by, bz)])

                return 0

            lax.fori_loop(0, 4, one, 0)

    def line(g, _):
        @pl.when(g == 0)
        def _():
            for j in range(4):
                pltpu.make_async_copy(w.at[j, x, y], w.at[j, x, y], w_recv.at[j]).wait()
            w_a1.start()
            w_b1.start()

        @pl.when(g == 2)
        def _():
            kv_a2.middle()
            kv_b2.middle()
            w_a1.middle()
            w_b1.middle()

        @pl.when(g == 4)
        def _():
            w_a1.finish()
            w_a2.start()
            w_b1.finish()
            w_b2.start()

        @pl.when(g == 6)
        def _():
            kv_a2.finish()
            kv_b2.finish()

        @pl.when(g == 7)
        def _():
            w_a2.middle()
            w_b2.middle()

        four(g)
        return 0

    lax.fori_loop(0, 8, line, 0)

    for h in range(8):
        att[:, :, h * HEAD_SIZE:(h + 1) * HEAD_SIZE] = (
            (acc[h] / tot[h]).astype(bf).reshape(2, 128, HEAD_SIZE)
        )
    w_a2.finish()
    w_b2.finish()

    half = remote(part_b, got, s_send, s_recv, {"exp": e + 1 - 2 * core})

    def project(rows, n):
        cols = pl.ds(pl.multiple_of(n * 256, 256), 256)
        return cols, jnp.dot(
            rows, w[:, :, :, :, cols].reshape(1024, 256), preferred_element_type=f32
        )

    def theirs(n, _):
        cols, value = project(att[1 - core], n)
        part_b[:, cols] = value.astype(bf)
        return 0

    def ours(n, _):
        cols, value = project(att[core], n)
        part_f[:, cols] = value
        return 0

    lax.fori_loop(0, 8, theirs, 0)
    half.start()
    lax.fori_loop(0, 8, ours, 0)
    half.wait_recv()
    hidden_s[...] = (part_f[...] + got[...].astype(f32)).astype(bf)

    hidden_f = hidden_s[...].astype(f32)
    inv_rms = lax.rsqrt(jnp.mean(hidden_f * hidden_f, axis=1, keepdims=True) + epsilon)
    for n in range(8):
        cols = slice(n * 256, (n + 1) * 256)
        unit = hidden_s[:, cols].astype(f32) * inv_rms
        dispatch(rows_s, (unit * gain_in[:, cols]).astype(bf), n)
    begin(rows_x)

    for copy in weight_copies:
        copy.wait()
    arrive(grads_x)
    cot = cr[...].reshape(SLOTS, DM)
    ct[...] = cot.T
    for n in range(3):
        cols = slice(n * 256, (n + 1) * 256)
        act_b[:, cols] = lax.dot_general(cot, wd[cols, :], over_last, preferred_element_type=f32)

    arrive(rows_x)
    rows = xr[...].reshape(SLOTS, DM)
    for n in range(3):
        cols = slice(n * 256, (n + 1) * 256)
        act_g[:, cols] = jnp.dot(rows, wg[:, cols], preferred_element_type=f32)
        act_u[:, cols] = jnp.dot(rows, wu[:, cols], preferred_element_type=f32)
    xt[...] = rows.T
    for n in range(3):
        cols = slice(n * 256, (n + 1) * 256)
        gate_act, up_act, back_units = act_g[:, cols], act_u[:, cols], act_b[:, cols]
        sigma = jax.nn.sigmoid(gate_act)
        gated = gate_act * sigma
        act[:, 1536 + n * 256:1536 + (n + 1) * 256] = (gated * up_act).astype(bf)
        act[:, cols] = (
            back_units * up_act * sigma * (1.0 + gate_act * (1.0 - sigma))
        ).astype(bf)
        act[:, 768 + n * 256:768 + (n + 1) * 256] = (back_units * gated).astype(bf)

    chains = []
    for c, (first, width) in enumerate(CHAINS):
        cols = pl.ds(first, width)
        wide = c < 2
        slots1 = (slots1_wide if wide else slots1_slim).at[c % 2]
        slots2 = (slots2_wide if wide else slots2_slim).at[c % 2]
        slot3 = (slot3_wide if wide else slot3_slim).at[c % 2]
        base = 13 * c
        if c % 2 == 0:
            one = RingSum(
                x, x_right, x_left, lambda i, h, cols=cols: grad.at[i, pl.ds(2 * h, 2), :, :, cols],
                slots1, rs_send, rs_recv, base, add_blocks)
            second = RingSum(
                y, y_right, y_left, lambda i, h, cols=cols: grad.at[x, i, h, :, cols],
                slots2, rs_send, rs_recv, base + 6, add_rows)
        else:
            one = RingSum(
                y, y_right, y_left, lambda i, h, cols=cols: grad.at[pl.ds(2 * h, 2), i, :, :, cols],
                slots1, rs_send, rs_recv, base, add_blocks)
            second = RingSum(
                x, x_right, x_left, lambda i, h, cols=cols: grad.at[i, y, h, :, cols],
                slots2, rs_send, rs_recv, base + 6, add_rows)
        last = remote(
            grad.at[x, y, 1 - z, :, cols], slot3,
            rs_send.at[base + 12], rs_recv.at[base + 12], z_partner,
        )
        chains.append((one, second, last, slot3))

    def weight_grads(step):
        px, py = wrap4(x + step), wrap4(y + step)
        for k in range(2):
            some = pl.ds(pl.multiple_of(px * 512 + k * 256, 256), 256)
            grad[px, 2 * k:2 * k + 2, :, :, 0:1152] = jnp.dot(
                xt[some, :], act[:, 0:1152], preferred_element_type=f32
            ).astype(bf).reshape(2, 2, 64, 1152)
        for k in range(4):
            some = pl.ds(pl.multiple_of(k * 512 + py * 128, 128), 128)
            grad[k, py, :, :, 1152:1536] = jnp.dot(
                xt[some, :], act[:, 1152:1536], preferred_element_type=f32
            ).astype(bf).reshape(2, 64, 384)
            grad[k, py, :, :, 1536:2304] = jnp.dot(
                ct[some, :], act[:, 1536:2304], preferred_element_type=f32
            ).astype(bf).reshape(2, 64, 768)

    def launch(*chosen):
        for chain in chains:
            chain[0].start(*chosen)

    weight_grads(2)
    launch(0, 1)
    for n in range(8):
        cols = slice(n * 256, (n + 1) * 256)
        res[:, :, cols] = jnp.dot(
            act[:, 1536:], wd[:, cols], preferred_element_type=f32
        ).astype(bf).reshape(8, CAP, 256)
    begin(res_x)
    weight_grads(1)
    launch(2)
    weight_grads(-1)
    launch(3)
    weight_grads(0)
    for n in range(8):
        cols = slice(n * 256, (n + 1) * 256)
        back[:, :, cols] = (
            lax.dot_general(act[:, 0:768], wg[cols, :], over_last, preferred_element_type=f32)
            + lax.dot_general(act[:, 768:1536], wu[cols, :], over_last, preferred_element_type=f32)
        ).astype(bf).reshape(8, CAP, 256)
    begin(back_x)

    for chain in chains:
        chain[0].middle()
    for chain in chains:
        chain[0].finish()
        chain[1].start()

    arrive(res_x)
    returned = res_r[...].reshape(SLOTS, DM)
    for n in range(8):
        cols = slice(n * 256, (n + 1) * 256)
        expert_sum = gates * jnp.dot(sel_t[...], returned[:, cols], preferred_element_type=f32)
        layer_out[:, cols] = (hidden_s[:, cols].astype(f32) + expert_sum).astype(bf)

    for chain in chains:
        chain[1].middle()
    for chain in chains:
        chain[1].finish()
        chain[2].start()

    arrive(back_x)
    returned = back_r[...].reshape(SLOTS, DM)
    shared = jnp.zeros((TOK, 1), f32)
    for n in range(8):
        cols = slice(n * 256, (n + 1) * 256)
        scaled = gain_in[:, cols] * jnp.dot(
            sel_t[...], returned[:, cols], preferred_element_type=f32
        )
        part_f[:, cols] = scaled
        unit = hidden_s[:, cols].astype(f32) * inv_rms
        shared = shared + jnp.sum(scaled * unit, axis=1, keepdims=True)
    shared = shared * (1.0 / DM)
    for n in range(8):
        cols = slice(n * 256, (n + 1) * 256)
        unit = hidden_s[:, cols].astype(f32) * inv_rms
        hidden_grad_out[:, cols] = (
            grad_in[:, cols].astype(f32) + inv_rms * (part_f[:, cols] - unit * shared)
        ).astype(bf)

    for (first, width), (_, _, last, slot3) in zip(CHAINS, chains):
        cols = slice(first, first + width)
        last.wait_recv()
        part_f[0:64, cols.start % 1152:cols.start % 1152 + width] = (
            grad[x, y, z, :, cols].astype(f32) + slot3[...].astype(f32)
        )
        if first == 0:
            gg_out[:, 0:640] = part_f[0:64, 0:640]
        elif first == 640:
            gg_out[:, 640:768] = part_f[0:64, 640:768]
            gu_out[:, 0:384] = part_f[0:64, 768:1152]
        elif first == 1152:
            gu_out[:, 384:768] = part_f[0:64, 0:384]
            gd_out[:, 0:256] = part_f[0:64, 384:640]
        else:
            gd_out[:, 256:768] = part_f[0:64, 640:1152]

    half.wait_send()
    z_copy.wait_send()
    for ring in (kv_a1, kv_b1, kv_a2, kv_b2, w_a1, w_b1, w_a2, w_b2):
        ring.drain()
    for n in range(2):
        @pl.when(jnp.logical_not(mine))
        def _():
            scatters[0][n].wait_send()

        for d in range(1, 4):
            scatters[d][n].wait_send()
    for one, second, last, _ in chains:
        one.drain()
        second.drain()
        last.wait_send()
    for pair in (rows_x, grads_x, res_x, back_x):
        for copy in pair[1]:
            copy.wait_send()


def on_device(
    queries, rotated_key_heads, value_head_rows, out_proj, norm_gain, expert_ids,
    gate_weights, expert_gate, expert_up, expert_down, grad_out,
):
    bf, f32 = jnp.bfloat16, jnp.float32
    anywhere = pl.BlockSpec(memory_space=pl.ANY)
    vmem = pl.BlockSpec(memory_space=pltpu.VMEM)
    dma = pltpu.SemaphoreType.DMA
    rows = jax.ShapeDtypeStruct((TOK, DM), bf)
    shard = jax.ShapeDtypeStruct((64, F), f32)
    swapped = pltpu.VMEM((8, CAP, DM), bf)
    units = pltpu.VMEM((SLOTS, F), f32)
    state = pltpu.VMEM((8, 256, HEAD_SIZE), f32)
    layer, hidden_grad, gg, gu, gd = pl.pallas_call(
        layer_kernel,
        out_shape=(rows, rows, shard, shard, shard),
        in_specs=[anywhere] * 4 + [vmem] * 3 + [anywhere] * 3 + [vmem],
        out_specs=(vmem,) * 5,
        scratch_shapes=[
            pltpu.VMEM((4, 256, 256), bf),
            pltpu.VMEM((4, 4, 2, 2, 256, HEAD_SIZE), bf),
            pltpu.VMEM((4, 4, 4, 16, DM), bf),
            state, state, state,
            pltpu.VMEM((2, 128, 1024), bf),
            pltpu.VMEM((TOK, DM), f32),
            pltpu.VMEM((TOK, DM), bf),
            pltpu.VMEM((TOK, DM), bf),
            pltpu.VMEM((SLOTS, TOK), bf),
            pltpu.VMEM((TOK, SLOTS), bf),
            pltpu.VMEM((TOK, DM), bf),
            swapped, swapped, swapped, swapped,
            pltpu.VMEM((DM, F), bf),
            pltpu.VMEM((DM, F), bf),
            pltpu.VMEM((F, DM), bf),
            units, units, units,
            pltpu.VMEM((SLOTS, 3 * F), bf),
            pltpu.VMEM((DM, SLOTS), bf),
            pltpu.VMEM((DM, SLOTS), bf),
            pltpu.VMEM((4, 4, 2, 64, 3 * F), bf),
            swapped, swapped, swapped, swapped,
            pltpu.VMEM((2, 6, 2, 2, 64, 640), bf),
            pltpu.VMEM((2, 6, 2, 2, 64, 512), bf),
            pltpu.VMEM((2, 6, 64, 640), bf),
            pltpu.VMEM((2, 6, 64, 512), bf),
            pltpu.VMEM((2, 64, 640), bf),
            pltpu.VMEM((2, 64, 512), bf),
            dma((5,)), dma((4,)), dma((4,)), dma((4,)), dma((4,)),
            dma(()), dma(()), dma((32,)), dma((32,)), dma(()), dma(()),
            dma((4,)), dma((4, 8)), dma((4, 8)), dma((52,)), dma((52,)),
        ],
        compiler_params=pltpu.CompilerParams(
            collective_id=1, has_side_effects=True, vmem_limit_bytes=62 * 1024 * 1024
        ),
        name="layer",
    )(
        queries, rotated_key_heads, value_head_rows, out_proj, norm_gain[None], expert_ids,
        gate_weights, expert_gate[0], expert_up[0], expert_down[0], grad_out,
    )
    return (layer, hidden_grad, gg[None], gu[None], gd.T[None])


def solution(mesh):
    in_specs = (
        P(None, "ctx", "exp"),
        P(None, "ctx", None),
        P(None, "ctx", None),
        P("exp", None),
        P(),
        P(("ctx", "exp"), None),
        P(("ctx", "exp"), None),
        P("exp", None, None),
        P("exp", None, None),
        P("exp", None, None),
        P(("ctx", "exp"), None),
    )
    out_specs = (
        P(("ctx", "exp"), None),
        P(("ctx", "exp"), None),
        P("exp", "ctx", None),
        P("exp", "ctx", None),
        P("exp", None, "ctx"),
    )
    return jax.shard_map(
        on_device, mesh=mesh, in_specs=in_specs, out_specs=out_specs, check_vma=False
    )
```

time: 228 us -> 174 us (0.76)
  Pallas kernels: 209 us -> 162 us
  matrix products: 7.92 us -> 0 us
  local copies, waits for them, and re-layouts: 6.4 us -> 11.4 us
  other arithmetic: 3.82 us -> 0 us
    pallas_call x2 -> x1, Pallas kernels: 209 us -> 162 us  [on_device(): pl.pallas_call(layer_kernel, out_shape=(rows, rows, shard, shard, shard),...]
    dot_general x4 -> x0, matrix products: 7.92 us -> none  [the longest x1 2.68 us: on_device(): jnp.dot(weighting.T, back_result.reshape(experts * capacity, dmodel).asty...]
    unnamed x23 -> x7, local copies, waits for them, and re-layouts: 6.4 us -> 11.4 us
where the time goes in v3:
time: 174 us
  Pallas kernels  162 us (93%)
  local copies, waits for them, and re-layouts  11.4 us (7%)
    pallas_call x1, Pallas kernels, on_device(): pl.pallas_call(layer_kernel, out_shape=(rows, rows, shard, shard, shard),...  162 us
    unnamed x7, local copies, waits for them, and re-layouts  11.4 us

profile of v3, /device:TPU:1, one launch (start us, length us, event | category | flops | bytes accessed | tf_op | source)
XLA Modules:
  0.0 173.6 jit_solution(14186485640700387152)
XLA Ops:
  0.6 1.4 copy.16.ids_in
  2.0 1.4 copy.17.weights_in
  3.4 161.6 %layer.1 = (bf16[128,2048]{1,0:T(8,128)(2,1)}, bf16[128,2048]{1,0:T(8,128)(2,1)}, f32[64,768]{1,0:T(8,128)}, f32[64,768]{1,0:T(8,128)}, f32[64,768]{1,0:T(8,128)}) custom-call(bf16[4,256,256]{2,1,0:T(8,128)(2,1)} %q_in.1, bf16[4,256,256]{2,1,0:T(8,128)(2,1)} %k_in.1, bf16[4,256,256]{2,1,0:T(8,128)(2,1)} %v_in.1, bf16[256,2048]{1,0:T(8,128)(2,1)} %o_in.1, ...), custom_call_target="tpu_custom_call" | custom-call | tf_op jit(solution)/shard_map/layer/pallas_call | solution.py:637
  165.0 1.9 %copy.23 = bf16[128,2048]{1,0:T(8,128)(2,1)} copy(bf16[128,2048]{1,0:T(8,128)(2,1)} %get-tuple-element.20) | data formatting | bytes 1048576
  166.9 1.9 %copy.24 = bf16[128,2048]{1,0:T(8,128)(2,1)} copy(bf16[128,2048]{1,0:T(8,128)(2,1)} %get-tuple-element.21) | data formatting | bytes 1048576
  168.8 1.6 copy.25
  170.4 1.6 copy.26
  172.0 1.6 copy.27

commit v4 on v3

--- a/solution.py
+++ b/solution.py
@@ -156,11 +156,11 @@
     q_in, k_in, v_in, o_in, gain_in, ids_in, weights_in, gate_in, up_in, down_in, grad_in,
     layer_out, hidden_grad_out, gg_out, gu_out, gd_out,
     qs, kv, w, best, tot, acc, att, part_f, part_b, got,
-    sel, sel_t, hidden_s, rows_s, grads_s, xr, cr, wg, wu, wd,
-    act_g, act_u, act_b, act, xt, ct, grad, res, back, res_r, back_r,
+    sel, sel_t, hidden_s, rows_s, grads_s, inv_s, inv_r, xr, cr, wg, wu, wd,
+    act_g, act_u, act_b, act, act_back, xt, ct, grad, res, back, res_r, back_r,
     slots1_wide, slots1_slim, slots2_wide, slots2_slim, slot3_wide, slot3_slim,
     lsem, q_send, q_recv, w_send, w_recv, z_send, z_recv, g_send, g_recv, s_send, s_recv,
-    a2a_local, a2a_send, a2a_recv, rs_send, rs_recv,
+    a2a_local, a2a_send, a2a_recv, r_local, r_send, r_recv, rs_send, rs_recv,
 ):
     ctx, e, x, y, z = mesh_place()
     f32, bf = jnp.float32, jnp.bfloat16
@@ -225,7 +225,7 @@
     mine = core == group
     own_q = pltpu.make_async_copy(q_in.at[seq], qs.at[slot], q_recv.at[slot])
     own_w = pltpu.make_async_copy(o_in.at[piece, :], w.at[slot, x, y], w_recv.at[slot])
-    for n, own in ((0, own_q), (1, own_w)):
+    for n, own in ((1, own_w), (0, own_q)):
         @pl.when(mine)
         def _():
             own.start()
@@ -272,33 +272,28 @@
         for copy in out:
             copy.wait_recv()
 
-    rows_x = exchange(rows_s, xr, 0)
     grads_x = exchange(grads_s, cr, 1)
     res_x = exchange(res, res_r, 2)
     back_x = exchange(back, back_r, 3)
 
     ids = ids_in[...]
-    lanes = lax.broadcasted_iota(jnp.int32, (TOK, TOK), 1)
-    chosen = (lanes == ids).astype(f32)
-    before = (lanes < lax.broadcasted_iota(jnp.int32, (TOK, TOK), 0)).astype(bf)
-    earlier = jnp.dot(before, chosen.astype(bf), preferred_element_type=f32)
-    place = ids.astype(f32) * CAP + jnp.sum(earlier * chosen, axis=1, keepdims=True)
-    slot_at = lax.broadcasted_iota(jnp.int32, (TOK, SLOTS), 1).astype(f32)
+    chosen = (lax.broadcasted_iota(jnp.int32, (16, TOK), 0) == ids).astype(f32)
+    rows_at = lax.broadcasted_iota(jnp.int32, (TOK, TOK), 0)
+    lanes_at = lax.broadcasted_iota(jnp.int32, (TOK, TOK), 1)
+    before = (rows_at < lanes_at).astype(bf)
+    earlier = jnp.dot(chosen.astype(bf), before, preferred_element_type=f32)
+    place = ids.astype(f32) * CAP + jnp.sum(earlier * chosen, axis=0, keepdims=True)
+    slot_at = lax.broadcasted_iota(jnp.int32, (SLOTS, TOK), 0).astype(f32)
     taken = (slot_at == place).astype(f32)
-    sel_t[...] = taken.astype(bf)
-    sel[...] = taken.T.astype(bf)
-    gates = weights_in[...]
-
-    def dispatch(dst, value, n):
-        cols = slice(n * 256, (n + 1) * 256)
-        dst[:, :, cols] = jnp.dot(
+    sel[...] = taken.astype(bf)
+    sel_t[...] = taken.T.astype(bf)
+    gates = jnp.sum(jnp.where(rows_at == lanes_at, weights_in[...], 0.0), axis=1, keepdims=True)
+
+    def dispatch(dst, value, first):
+        width = value.shape[1]
+        dst[:, :, first:first + width] = jnp.dot(
             sel[...], value, preferred_element_type=f32
-        ).astype(bf).reshape(8, CAP, 256)
-
-    for n in range(8):
-        cols = slice(n * 256, (n + 1) * 256)
-        dispatch(grads_s, (grad_in[:, cols].astype(f32) * gates).astype(bf), n)
-    begin(grads_x)
+        ).astype(bf).reshape(8, CAP, width)
 
     kv_a1.middle()
     kv_b1.middle()
@@ -306,6 +301,14 @@
     kv_a2.start()
     kv_b1.finish()
     kv_b2.start()
+    for j in range(4):
+        pltpu.make_async_copy(w.at[j, x, y], w.at[j, x, y], w_recv.at[j]).wait()
+    w_a1.start()
+    w_b1.start()
+    for n in range(8):
+        cols = slice(n * 256, (n + 1) * 256)
+        dispatch(grads_s, (grad_in[:, cols].astype(f32) * gates).astype(bf), n * 256)
+    begin(grads_x)
     for j in range(4):
         pltpu.make_async_copy(qs.at[j], qs.at[j], q_recv.at[j]).wait()
 
@@ -374,26 +377,17 @@
 
             lax.fori_loop(0, 4, one, 0)
 
+    w_a1.middle()
+    w_b1.middle()
+
     def line(g, _):
-        @pl.when(g == 0)
-        def _():
-            for j in range(4):
-                pltpu.make_async_copy(w.at[j, x, y], w.at[j, x, y], w_recv.at[j]).wait()
-            w_a1.start()
-            w_b1.start()
-
         @pl.when(g == 2)
         def _():
+            w_a1.finish()
+            w_b1.finish()
             kv_a2.middle()
             kv_b2.middle()
-            w_a1.middle()
-            w_b1.middle()
-
-        @pl.when(g == 4)
-        def _():
-            w_a1.finish()
             w_a2.start()
-            w_b1.finish()
             w_b2.start()
 
         @pl.when(g == 6)
@@ -418,37 +412,52 @@
     w_a2.finish()
     w_b2.finish()
 
-    half = remote(part_b, got, s_send, s_recv, {"exp": e + 1 - 2 * core})
-
-    def project(rows, n):
-        cols = pl.ds(pl.multiple_of(n * 256, 256), 256)
-        return cols, jnp.dot(
-            rows, w[:, :, :, :, cols].reshape(1024, 256), preferred_element_type=f32
+    sibling = {"exp": e + 1 - 2 * core}
+    halves, row_copies = [], []
+    for n in range(4):
+        cols = pl.ds(n * 512, 512)
+        halves.append(remote(
+            part_b.at[:, cols], got.at[:, cols], s_send.at[n], s_recv.at[n], sibling
+        ))
+        own_rows = pltpu.make_async_copy(
+            rows_s.at[e, :, cols], xr.at[e, :, cols], r_local.at[n]
         )
-
-    def theirs(n, _):
-        cols, value = project(att[1 - core], n)
-        part_b[:, cols] = value.astype(bf)
-        return 0
-
-    def ours(n, _):
-        cols, value = project(att[core], n)
-        part_f[:, cols] = value
-        return 0
-
-    lax.fori_loop(0, 8, theirs, 0)
-    half.start()
-    lax.fori_loop(0, 8, ours, 0)
-    half.wait_recv()
-    hidden_s[...] = (part_f[...] + got[...].astype(f32)).astype(bf)
-
-    hidden_f = hidden_s[...].astype(f32)
-    inv_rms = lax.rsqrt(jnp.mean(hidden_f * hidden_f, axis=1, keepdims=True) + epsilon)
-    for n in range(8):
-        cols = slice(n * 256, (n + 1) * 256)
-        unit = hidden_s[:, cols].astype(f32) * inv_rms
-        dispatch(rows_s, (unit * gain_in[:, cols]).astype(bf), n)
-    begin(rows_x)
+        out = []
+        for d in range(1, 8):
+            to = lax.rem(e + d, 8)
+            out.append(remote(
+                rows_s.at[to, :, cols], xr.at[e, :, cols],
+                r_send.at[n, d], r_recv.at[n, d], {"exp": to},
+            ))
+        row_copies.append((own_rows, out))
+
+    def project(rows, first):
+        return jnp.dot(
+            rows, w[:, :, :, :, first:first + 256].reshape(1024, 256), preferred_element_type=f32
+        )
+
+    for n in range(4):
+        for first in (n * 512, n * 512 + 256):
+            part_b[:, first:first + 256] = project(att[1 - core], first).astype(bf)
+        halves[n].start()
+    squares = jnp.zeros((TOK, 1), f32)
+    for n in range(4):
+        cols = slice(n * 512, (n + 1) * 512)
+        for first in (n * 512, n * 512 + 256):
+            part_f[:, first:first + 256] = project(att[core], first)
+        halves[n].wait_recv()
+        hidden = (part_f[:, cols] + got[:, cols].astype(f32)).astype(bf)
+        hidden_s[:, cols] = hidden
+        hidden = hidden.astype(f32)
+        squares = squares + jnp.sum(hidden * hidden, axis=1, keepdims=True)
+        dispatch(rows_s, (hidden * gain_in[:, cols]).astype(bf), n * 512)
+        begin(row_copies[n])
+    inv_rms = lax.rsqrt(squares * (1.0 / DM) + epsilon)
+    inv_row = jnp.broadcast_to(inv_rms, (TOK, TOK)).T[0:1, :]
+    inv_slots = jnp.sum(sel[...].astype(f32) * inv_row, axis=1, keepdims=True)
+    inv_s[...] = jnp.broadcast_to(inv_slots, (SLOTS, 128)).reshape(8, CAP, 128)
+    inv_x = exchange(inv_s, inv_r, 0)
+    begin(inv_x)
 
     for copy in weight_copies:
         copy.wait()
@@ -459,12 +468,15 @@
         cols = slice(n * 256, (n + 1) * 256)
         act_b[:, cols] = lax.dot_general(cot, wd[cols, :], over_last, preferred_element_type=f32)
 
-    arrive(rows_x)
+    for pair in row_copies:
+        arrive(pair)
+    arrive(inv_x)
+    inv_in = inv_r[...].reshape(SLOTS, 128)[:, 0:1]
     rows = xr[...].reshape(SLOTS, DM)
     for n in range(3):
         cols = slice(n * 256, (n + 1) * 256)
-        act_g[:, cols] = jnp.dot(rows, wg[:, cols], preferred_element_type=f32)
-        act_u[:, cols] = jnp.dot(rows, wu[:, cols], preferred_element_type=f32)
+        act_g[:, cols] = jnp.dot(rows, wg[:, cols], preferred_element_type=f32) * inv_in
+        act_u[:, cols] = jnp.dot(rows, wu[:, cols], preferred_element_type=f32) * inv_in
     xt[...] = rows.T
     for n in range(3):
         cols = slice(n * 256, (n + 1) * 256)
@@ -472,10 +484,12 @@
         sigma = jax.nn.sigmoid(gate_act)
         gated = gate_act * sigma
         act[:, 1536 + n * 256:1536 + (n + 1) * 256] = (gated * up_act).astype(bf)
-        act[:, cols] = (
-            back_units * up_act * sigma * (1.0 + gate_act * (1.0 - sigma))
-        ).astype(bf)
-        act[:, 768 + n * 256:768 + (n + 1) * 256] = (back_units * gated).astype(bf)
+        back_gate = back_units * up_act * sigma * (1.0 + gate_act * (1.0 - sigma))
+        back_up = back_units * gated
+        act[:, cols] = (back_gate * inv_in).astype(bf)
+        act[:, 768 + n * 256:768 + (n + 1) * 256] = (back_up * inv_in).astype(bf)
+        act_back[:, cols] = back_gate.astype(bf)
+        act_back[:, 768 + n * 256:768 + (n + 1) * 256] = back_up.astype(bf)
 
     chains = []
     for c, (first, width) in enumerate(CHAINS):
@@ -541,8 +555,8 @@
     for n in range(8):
         cols = slice(n * 256, (n + 1) * 256)
         back[:, :, cols] = (
-            lax.dot_general(act[:, 0:768], wg[cols, :], over_last, preferred_element_type=f32)
-            + lax.dot_general(act[:, 768:1536], wu[cols, :], over_last, preferred_element_type=f32)
+            lax.dot_general(act_back[:, 0:768], wg[cols, :], over_last, preferred_element_type=f32)
+            + lax.dot_general(act_back[:, 768:1536], wu[cols, :], over_last, preferred_element_type=f32)
         ).astype(bf).reshape(8, CAP, 256)
     begin(back_x)
 
@@ -601,7 +615,8 @@
         else:
             gd_out[:, 256:768] = part_f[0:64, 640:1152]
 
-    half.wait_send()
+    for half in halves:
+        half.wait_send()
     z_copy.wait_send()
     for ring in (kv_a1, kv_b1, kv_a2, kv_b2, w_a1, w_b1, w_a2, w_b2):
         ring.drain()
@@ -616,9 +631,21 @@
         one.drain()
         second.drain()
         last.wait_send()
-    for pair in (rows_x, grads_x, res_x, back_x):
+    for pair in row_copies + [inv_x, grads_x, res_x, back_x]:
         for copy in pair[1]:
             copy.wait_send()
+
+
+def hand_over(*refs):
+    sems = refs[10]
+    copies = [
+        pltpu.make_async_copy(src, dst, sems.at[n])
+        for n, (src, dst) in enumerate(zip(refs[:5], refs[5:10]))
+    ]
+    for copy in copies:
+        copy.start()
+    for copy in copies:
+        copy.wait()
 
 
 def on_device(
@@ -651,12 +678,16 @@
             pltpu.VMEM((SLOTS, TOK), bf),
             pltpu.VMEM((TOK, SLOTS), bf),
             pltpu.VMEM((TOK, DM), bf),
-            swapped, swapped, swapped, swapped,
+            swapped, swapped,
+            pltpu.VMEM((8, CAP, 128), f32),
+            pltpu.VMEM((8, CAP, 128), f32),
+            swapped, swapped,
             pltpu.VMEM((DM, F), bf),
             pltpu.VMEM((DM, F), bf),
             pltpu.VMEM((F, DM), bf),
             units, units, units,
             pltpu.VMEM((SLOTS, 3 * F), bf),
+            pltpu.VMEM((SLOTS, 2 * F), bf),
             pltpu.VMEM((DM, SLOTS), bf),
             pltpu.VMEM((DM, SLOTS), bf),
             pltpu.VMEM((4, 4, 2, 64, 3 * F), bf),
@@ -668,17 +699,28 @@
             pltpu.VMEM((2, 64, 640), bf),
             pltpu.VMEM((2, 64, 512), bf),
             dma((5,)), dma((4,)), dma((4,)), dma((4,)), dma((4,)),
-            dma(()), dma(()), dma((32,)), dma((32,)), dma(()), dma(()),
-            dma((4,)), dma((4, 8)), dma((4, 8)), dma((52,)), dma((52,)),
+            dma(()), dma(()), dma((32,)), dma((32,)), dma((4,)), dma((4,)),
+            dma((4,)), dma((4, 8)), dma((4, 8)), dma((4,)), dma((4, 8)), dma((4, 8)),
+            dma((52,)), dma((52,)),
         ],
         compiler_params=pltpu.CompilerParams(
             collective_id=1, has_side_effects=True, vmem_limit_bytes=62 * 1024 * 1024
         ),
         name="layer",
     )(
-        queries, rotated_key_heads, value_head_rows, out_proj, norm_gain[None], expert_ids,
-        gate_weights, expert_gate[0], expert_up[0], expert_down[0], grad_out,
+        queries, rotated_key_heads, value_head_rows, out_proj, norm_gain[None],
+        expert_ids.reshape(1, TOK), gate_weights.reshape(1, TOK), expert_gate[0], expert_up[0], expert_down[0], grad_out,
     )
+    shapes = (rows, rows, shard, shard, shard)
+    layer, hidden_grad, gg, gu, gd = pl.pallas_call(
+        hand_over,
+        out_shape=shapes,
+        in_specs=[anywhere] * 5,
+        out_specs=[anywhere] * 5,
+        scratch_shapes=[dma((5,))],
+        compiler_params=pltpu.CompilerParams(vmem_limit_bytes=62 * 1024 * 1024),
+        name="hand_over",
+    )(layer, hidden_grad, gg, gu, gd)
     return (layer, hidden_grad, gg[None], gu[None], gd.T[None])
 
 

time: 174 us -> 219 us (1.26)
  Pallas kernels: 162 us -> 218 us
  local copies, waits for them, and re-layouts: 11.4 us -> 0 us
    pallas_call x0 -> x1, Pallas kernels: none -> 50.8 us  [on_device(): pl.pallas_call(hand_over, out_shape=shapes, in_specs=[anywhere] * 5, out_...]
    unnamed x7 -> x0, local copies, waits for them, and re-layouts: 11.4 us -> none
    pallas_call x1, Pallas kernels: 162 us -> 167 us  [on_device(): pl.pallas_call(layer_kernel, out_shape=(rows, rows, shard, shard, shard),...]
where the time goes in v4:
time: 219 us
  Pallas kernels  218 us (100%)
    pallas_call x1, Pallas kernels, on_device(): pl.pallas_call(layer_kernel, out_shape=(rows, rows, shard, shard, shard),...  167 us
    pallas_call x1, Pallas kernels, on_device(): pl.pallas_call(hand_over, out_shape=shapes, in_specs=[anywhere] * 5, out_...  50.8 us

profile of v4, /device:TPU:1, one launch (start us, length us, event | category | flops | bytes accessed | tf_op | source)
XLA Modules:
  0.0 218.9 jit_solution(1713953131937983089)
XLA Ops:
  0.6 167.3 %layer.1 = (bf16[128,2048]{1,0:T(8,128)(2,1)}, bf16[128,2048]{1,0:T(8,128)(2,1)}, f32[64,768]{1,0:T(8,128)}, f32[64,768]{1,0:T(8,128)}, f32[64,768]{1,0:T(8,128)}) custom-call(bf16[4,256,256]{2,1,0:T(8,128)(2,1)} %q_in.1, bf16[4,256,256]{2,1,0:T(8,128)(2,1)} %k_in.1, bf16[4,256,256]{2,1,0:T(8,128)(2,1)} %v_in.1, bf16[256,2048]{1,0:T(8,128)(2,1)} %o_in.1, ...), custom_call_target="tpu_custom_call" | custom-call | tf_op jit(solution)/shard_map/layer/pallas_call | solution.py:664
  167.9 50.8 %hand_over.1 = (bf16[128,2048]{1,0:T(8,128)(2,1)}, bf16[128,2048]{1,0:T(8,128)(2,1)}, f32[64,768]{1,0:T(8,128)}, f32[64,768]{1,0:T(8,128)}, f32[64,768]{1,0:T(8,128)}) custom-call(bf16[128,2048]{1,0:T(8,128)(2,1)} %get-tuple-element.15.refs_0_, bf16[128,2048]{1,0:T(8,128)(2,1)} %get-tuple-element.16.refs_1_, f32[64,768]{1,0:T(8,128)} %get-tuple-element.17.refs_2_, ...), custom_call_target="tpu_custom_call" | custom-call | tf_op jit(solution)/shard_map/hand_over/pallas_call | solution.py:715

commit v5 on v4

--- a/solution.py
+++ b/solution.py
@@ -193,10 +193,19 @@
     kv_b1 = ring_y(4, lambda i, h: kv.at[x, i, 1] if h is None else kv.at[x, i, 1, h])
     kv_a2 = ring_y(8, lambda i, h: kv.at[two(h), i, 0])
     kv_b2 = ring_x(12, lambda i, h: kv.at[i, two(h), 1])
-    w_a1 = ring_x(16, lambda i, h: w.at[pl.ds(0, 2), i, y] if h is None else w.at[h, i, y])
-    w_b1 = ring_y(20, lambda i, h: w.at[pl.ds(2, 2), x, i] if h is None else w.at[2 + h, x, i])
-    w_a2 = ring_y(24, lambda i, h: w.at[pl.ds(0, 2), :, i] if h is None else w.at[h, :, i])
-    w_b2 = ring_x(28, lambda i, h: w.at[pl.ds(2, 2), i] if h is None else w.at[2 + h, i])
+    w_rings = []
+    for c in range(2):
+        cw = w.at[c]
+        w_rings.append((
+            ring_x(16 + 16 * c, lambda i, h, cw=cw: (
+                cw.at[pl.ds(0, 2), i, y] if h is None else cw.at[h, i, y])),
+            ring_y(20 + 16 * c, lambda i, h, cw=cw: (
+                cw.at[pl.ds(2, 2), x, i] if h is None else cw.at[2 + h, x, i])),
+            ring_y(24 + 16 * c, lambda i, h, cw=cw: (
+                cw.at[pl.ds(0, 2), :, i] if h is None else cw.at[h, :, i])),
+            ring_x(28 + 16 * c, lambda i, h, cw=cw: (
+                cw.at[pl.ds(2, 2), i] if h is None else cw.at[2 + h, i])),
+        ))
     z_partner = {"ctx": ctx_of(x, y, 1 - z)}
     z_copy = remote(kv.at[x, y, z], kv.at[x, y, z], z_send, z_recv, z_partner)
 
@@ -216,19 +225,29 @@
     scatters = []
     for d in range(4):
         to = {"exp": 2 * lax.rem(seq + d, 4) + group}
-        scatters.append((
+        sends = [
             remote(
-                q_in.at[lax.rem(seq + d, 4)], qs.at[slot], q_send.at[d], q_recv.at[slot], to
-            ),
-            remote(o_in.at[piece, :], w.at[slot, x, y], w_send.at[d], w_recv.at[slot], to),
+                o_in.at[piece, pl.ds(c * 1024, 1024)], w.at[c, slot, x, y],
+                w_send.at[c, d], w_recv.at[c, slot], to,
+            )
+            for c in range(2)
+        ]
+        sends.append(remote(
+            q_in.at[lax.rem(seq + d, 4)], qs.at[slot], q_send.at[d], q_recv.at[slot], to
         ))
+        scatters.append(sends)
     mine = core == group
-    own_q = pltpu.make_async_copy(q_in.at[seq], qs.at[slot], q_recv.at[slot])
-    own_w = pltpu.make_async_copy(o_in.at[piece, :], w.at[slot, x, y], w_recv.at[slot])
-    for n, own in ((1, own_w), (0, own_q)):
+    own_pieces = [
+        pltpu.make_async_copy(
+            o_in.at[piece, pl.ds(c * 1024, 1024)], w.at[c, slot, x, y], w_recv.at[c, slot]
+        )
+        for c in range(2)
+    ]
+    own_pieces.append(pltpu.make_async_copy(q_in.at[seq], qs.at[slot], q_recv.at[slot]))
+    for n in range(3):
         @pl.when(mine)
         def _():
-            own.start()
+            own_pieces[n].start()
 
         @pl.when(jnp.logical_not(mine))
         def _():
@@ -301,16 +320,24 @@
     kv_a2.start()
     kv_b1.finish()
     kv_b2.start()
-    for j in range(4):
-        pltpu.make_async_copy(w.at[j, x, y], w.at[j, x, y], w_recv.at[j]).wait()
-    w_a1.start()
-    w_b1.start()
+    for c in range(2):
+        for j in range(4):
+            pltpu.make_async_copy(w.at[c, j, x, y], w.at[c, j, x, y], w_recv.at[c, j]).wait()
+        for ring in w_rings[c][:2]:
+            ring.start()
     for n in range(8):
         cols = slice(n * 256, (n + 1) * 256)
         dispatch(grads_s, (grad_in[:, cols].astype(f32) * gates).astype(bf), n * 256)
-    begin(grads_x)
+    for c in range(2):
+        for ring in w_rings[c][:2]:
+            ring.middle()
+    for ring in w_rings[0][:2]:
+        ring.finish()
+    for ring in w_rings[0][2:]:
+        ring.start()
     for j in range(4):
         pltpu.make_async_copy(qs.at[j], qs.at[j], q_recv.at[j]).wait()
+    begin(grads_x)
 
     scale = math.log2(math.e) / math.sqrt(HEAD_SIZE)
     over_last = (((1,), (1,)), ((), ()))
@@ -377,29 +404,26 @@
 
             lax.fori_loop(0, 4, one, 0)
 
-    w_a1.middle()
-    w_b1.middle()
-
     def line(g, _):
         @pl.when(g == 2)
         def _():
-            w_a1.finish()
-            w_b1.finish()
             kv_a2.middle()
             kv_b2.middle()
-            w_a2.start()
-            w_b2.start()
+            for ring in w_rings[1][:2]:
+                ring.finish()
+            for ring in w_rings[1][2:]:
+                ring.start()
+
+        @pl.when(g == 4)
+        def _():
+            for ring in w_rings[0][2:]:
+                ring.middle()
 
         @pl.when(g == 6)
         def _():
             kv_a2.finish()
             kv_b2.finish()
 
-        @pl.when(g == 7)
-        def _():
-            w_a2.middle()
-            w_b2.middle()
-
         four(g)
         return 0
 
@@ -409,8 +433,6 @@
         att[:, :, h * HEAD_SIZE:(h + 1) * HEAD_SIZE] = (
             (acc[h] / tot[h]).astype(bf).reshape(2, 128, HEAD_SIZE)
         )
-    w_a2.finish()
-    w_b2.finish()
 
     sibling = {"exp": e + 1 - 2 * core}
     halves, row_copies = [], []
@@ -433,25 +455,32 @@
 
     def project(rows, first):
         return jnp.dot(
-            rows, w[:, :, :, :, first:first + 256].reshape(1024, 256), preferred_element_type=f32
+            rows, w[first // 1024, :, :, :, :, first % 1024:first % 1024 + 256].reshape(1024, 256),
+            preferred_element_type=f32,
         )
 
-    for n in range(4):
-        for first in (n * 512, n * 512 + 256):
-            part_b[:, first:first + 256] = project(att[1 - core], first).astype(bf)
-        halves[n].start()
     squares = jnp.zeros((TOK, 1), f32)
-    for n in range(4):
-        cols = slice(n * 512, (n + 1) * 512)
-        for first in (n * 512, n * 512 + 256):
-            part_f[:, first:first + 256] = project(att[core], first)
-        halves[n].wait_recv()
-        hidden = (part_f[:, cols] + got[:, cols].astype(f32)).astype(bf)
-        hidden_s[:, cols] = hidden
-        hidden = hidden.astype(f32)
-        squares = squares + jnp.sum(hidden * hidden, axis=1, keepdims=True)
-        dispatch(rows_s, (hidden * gain_in[:, cols]).astype(bf), n * 512)
-        begin(row_copies[n])
+    for c in range(2):
+        for ring in w_rings[c][2:]:
+            if c == 1:
+                ring.middle()
+        for ring in w_rings[c][2:]:
+            ring.finish()
+        for n in (2 * c, 2 * c + 1):
+            for first in (n * 512, n * 512 + 256):
+                part_b[:, first:first + 256] = project(att[1 - core], first).astype(bf)
+            halves[n].start()
+        for n in (2 * c, 2 * c + 1):
+            cols = slice(n * 512, (n + 1) * 512)
+            for first in (n * 512, n * 512 + 256):
+                part_f[:, first:first + 256] = project(att[core], first)
+            halves[n].wait_recv()
+            hidden = (part_f[:, cols] + got[:, cols].astype(f32)).astype(bf)
+            hidden_s[:, cols] = hidden
+            hidden = hidden.astype(f32)
+            squares = squares + jnp.sum(hidden * hidden, axis=1, keepdims=True)
+            dispatch(rows_s, (hidden * gain_in[:, cols]).astype(bf), n * 512)
+            begin(row_copies[n])
     inv_rms = lax.rsqrt(squares * (1.0 / DM) + epsilon)
     inv_row = jnp.broadcast_to(inv_rms, (TOK, TOK)).T[0:1, :]
     inv_slots = jnp.sum(sel[...].astype(f32) * inv_row, axis=1, keepdims=True)
@@ -566,18 +595,18 @@
         chain[0].finish()
         chain[1].start()
 
-    arrive(res_x)
-    returned = res_r[...].reshape(SLOTS, DM)
-    for n in range(8):
-        cols = slice(n * 256, (n + 1) * 256)
-        expert_sum = gates * jnp.dot(sel_t[...], returned[:, cols], preferred_element_type=f32)
-        layer_out[:, cols] = (hidden_s[:, cols].astype(f32) + expert_sum).astype(bf)
-
     for chain in chains:
         chain[1].middle()
     for chain in chains:
         chain[1].finish()
         chain[2].start()
+
+    arrive(res_x)
+    returned = res_r[...].reshape(SLOTS, DM)
+    for n in range(8):
+        cols = slice(n * 256, (n + 1) * 256)
+        expert_sum = gates * jnp.dot(sel_t[...], returned[:, cols], preferred_element_type=f32)
+        layer_out[:, cols] = (hidden_s[:, cols].astype(f32) + expert_sum).astype(bf)
 
     arrive(back_x)
     returned = back_r[...].reshape(SLOTS, DM)
@@ -618,9 +647,9 @@
     for half in halves:
         half.wait_send()
     z_copy.wait_send()
-    for ring in (kv_a1, kv_b1, kv_a2, kv_b2, w_a1, w_b1, w_a2, w_b2):
+    for ring in [kv_a1, kv_b1, kv_a2, kv_b2] + list(w_rings[0]) + list(w_rings[1]):
         ring.drain()
-    for n in range(2):
+    for n in range(3):
         @pl.when(jnp.logical_not(mine))
         def _():
             scatters[0][n].wait_send()
@@ -637,15 +666,8 @@
 
 
 def hand_over(*refs):
-    sems = refs[10]
-    copies = [
-        pltpu.make_async_copy(src, dst, sems.at[n])
-        for n, (src, dst) in enumerate(zip(refs[:5], refs[5:10]))
-    ]
-    for copy in copies:
-        copy.start()
-    for copy in copies:
-        copy.wait()
+    for src, dst in zip(refs[:5], refs[5:]):
+        dst[...] = src[...]
 
 
 def on_device(
@@ -669,7 +691,7 @@
         scratch_shapes=[
             pltpu.VMEM((4, 256, 256), bf),
             pltpu.VMEM((4, 4, 2, 2, 256, HEAD_SIZE), bf),
-            pltpu.VMEM((4, 4, 4, 16, DM), bf),
+            pltpu.VMEM((2, 4, 4, 4, 16, 1024), bf),
             state, state, state,
             pltpu.VMEM((2, 128, 1024), bf),
             pltpu.VMEM((TOK, DM), f32),
@@ -698,8 +720,8 @@
             pltpu.VMEM((2, 6, 64, 512), bf),
             pltpu.VMEM((2, 64, 640), bf),
             pltpu.VMEM((2, 64, 512), bf),
-            dma((5,)), dma((4,)), dma((4,)), dma((4,)), dma((4,)),
-            dma(()), dma(()), dma((32,)), dma((32,)), dma((4,)), dma((4,)),
+            dma((5,)), dma((4,)), dma((4,)), dma((2, 4)), dma((2, 4)),
+            dma(()), dma(()), dma((48,)), dma((48,)), dma((4,)), dma((4,)),
             dma((4,)), dma((4, 8)), dma((4, 8)), dma((4,)), dma((4, 8)), dma((4, 8)),
             dma((52,)), dma((52,)),
         ],
@@ -715,9 +737,8 @@
     layer, hidden_grad, gg, gu, gd = pl.pallas_call(
         hand_over,
         out_shape=shapes,
-        in_specs=[anywhere] * 5,
-        out_specs=[anywhere] * 5,
-        scratch_shapes=[dma((5,))],
+        in_specs=[vmem] * 5,
+        out_specs=[vmem] * 5,
         compiler_params=pltpu.CompilerParams(vmem_limit_bytes=62 * 1024 * 1024),
         name="hand_over",
     )(layer, hidden_grad, gg, gu, gd)

time: 219 us -> 168 us (0.77)
  Pallas kernels: 218 us -> 166 us
    pallas_call x1, Pallas kernels: 50.8 us -> 2.55 us  [on_device(): pl.pallas_call(hand_over, out_shape=shapes, in_specs=[vmem] * 5, out_spec...]
    pallas_call x1, Pallas kernels: 167 us -> 164 us  [on_device(): pl.pallas_call(layer_kernel, out_shape=(rows, rows, shard, shard, shard),...]
where the time goes in v5:
time: 168 us; the launch traced here: 167 us
  Pallas kernels  166 us (99%)
    pallas_call x1, Pallas kernels, on_device(): pl.pallas_call(layer_kernel, out_shape=(rows, rows, shard, shard, shard),...  164 us

profile of v5, /device:TPU:1, one launch (start us, length us, event | category | flops | bytes accessed | tf_op | source)
XLA Modules:
  0.0 166.7 jit_solution(88938935565671630)
XLA Ops:
  0.6 163.5 %layer.1 = (bf16[128,2048]{1,0:T(8,128)(2,1)}, bf16[128,2048]{1,0:T(8,128)(2,1)}, f32[64,768]{1,0:T(8,128)}, f32[64,768]{1,0:T(8,128)}, f32[64,768]{1,0:T(8,128)}) custom-call(bf16[4,256,256]{2,1,0:T(8,128)(2,1)} %q_in.1, bf16[4,256,256]{2,1,0:T(8,128)(2,1)} %k_in.1, bf16[4,256,256]{2,1,0:T(8,128)(2,1)} %v_in.1, bf16[256,2048]{1,0:T(8,128)(2,1)} %o_in.1, ...), custom_call_target="tpu_custom_call" | custom-call | tf_op jit(solution)/shard_map/layer/pallas_call | solution.py:686
  164.2 2.5 %hand_over.1 = (bf16[128,2048]{1,0:T(8,128)(2,1)}, bf16[128,2048]{1,0:T(8,128)(2,1)}, f32[64,768]{1,0:T(8,128)}, f32[64,768]{1,0:T(8,128)}, f32[64,768]{1,0:T(8,128)}) custom-call(bf16[128,2048]{1,0:T(8,128)(2,1)} %get-tuple-element.15.refs_0_, bf16[128,2048]{1,0:T(8,128)(2,1)} %get-tuple-element.16.refs_1_, f32[64,768]{1,0:T(8,128)} %get-tuple-element.17.refs_2_, ...), custom_call_target="tpu_custom_call" | custom-call | tf_op jit(solution)/shard_map/hand_over/pallas_call | solution.py:737

commit v6 on v5

--- a/solution.py
+++ b/solution.py
@@ -244,7 +244,7 @@
         for c in range(2)
     ]
     own_pieces.append(pltpu.make_async_copy(q_in.at[seq], qs.at[slot], q_recv.at[slot]))
-    for n in range(3):
+    for n in (2, 0, 1):
         @pl.when(mine)
         def _():
             own_pieces[n].start()
@@ -409,15 +409,15 @@
         def _():
             kv_a2.middle()
             kv_b2.middle()
+
+        @pl.when(g == 4)
+        def _():
+            for ring in w_rings[0][2:]:
+                ring.middle()
             for ring in w_rings[1][:2]:
                 ring.finish()
             for ring in w_rings[1][2:]:
                 ring.start()
-
-        @pl.when(g == 4)
-        def _():
-            for ring in w_rings[0][2:]:
-                ring.middle()
 
         @pl.when(g == 6)
         def _():
@@ -497,19 +497,28 @@
         cols = slice(n * 256, (n + 1) * 256)
         act_b[:, cols] = lax.dot_general(cot, wd[cols, :], over_last, preferred_element_type=f32)
 
-    for pair in row_copies:
-        arrive(pair)
+    for c in range(2):
+        for pair in row_copies[2 * c:2 * c + 2]:
+            arrive(pair)
+        part = slice(c * 1024, (c + 1) * 1024)
+        rows = xr[:, :, part].reshape(SLOTS, 1024)
+        for n in range(3):
+            cols = slice(n * 256, (n + 1) * 256)
+            gate_part = jnp.dot(rows, wg[part, cols], preferred_element_type=f32)
+            up_part = jnp.dot(rows, wu[part, cols], preferred_element_type=f32)
+            if c == 0:
+                act_g[:, cols] = gate_part
+                act_u[:, cols] = up_part
+            else:
+                act_g[:, cols] = act_g[:, cols] + gate_part
+                act_u[:, cols] = act_u[:, cols] + up_part
+        xt[part, :] = rows.T
     arrive(inv_x)
     inv_in = inv_r[...].reshape(SLOTS, 128)[:, 0:1]
-    rows = xr[...].reshape(SLOTS, DM)
     for n in range(3):
         cols = slice(n * 256, (n + 1) * 256)
-        act_g[:, cols] = jnp.dot(rows, wg[:, cols], preferred_element_type=f32) * inv_in
-        act_u[:, cols] = jnp.dot(rows, wu[:, cols], preferred_element_type=f32) * inv_in
-    xt[...] = rows.T
-    for n in range(3):
-        cols = slice(n * 256, (n + 1) * 256)
-        gate_act, up_act, back_units = act_g[:, cols], act_u[:, cols], act_b[:, cols]
+        gate_act, up_act = act_g[:, cols] * inv_in, act_u[:, cols] * inv_in
+        back_units = act_b[:, cols]
         sigma = jax.nn.sigmoid(gate_act)
         gated = gate_act * sigma
         act[:, 1536 + n * 256:1536 + (n + 1) * 256] = (gated * up_act).astype(bf)

time: 168 us -> 169 us (level)
  Pallas kernels: 166 us -> 168 us
    pallas_call x1, Pallas kernels: 164 us -> 166 us  [on_device(): pl.pallas_call(layer_kernel, out_shape=(rows, rows, shard, shard, shard),...]
where the time goes in v6:
time: 169 us
  Pallas kernels  168 us (99%)
    pallas_call x1, Pallas kernels, on_device(): pl.pallas_call(layer_kernel, out_shape=(rows, rows, shard, shard, shard),...  166 us

profile of v6, /device:TPU:1, one launch (start us, length us, event | category | flops | bytes accessed | tf_op | source)
XLA Modules:
  0.0 169.0 jit_solution(15160766100551861865)
XLA Ops:
  0.6 165.8 %layer.1 = (bf16[128,2048]{1,0:T(8,128)(2,1)}, bf16[128,2048]{1,0:T(8,128)(2,1)}, f32[64,768]{1,0:T(8,128)}, f32[64,768]{1,0:T(8,128)}, f32[64,768]{1,0:T(8,128)}) custom-call(bf16[4,256,256]{2,1,0:T(8,128)(2,1)} %q_in.1, bf16[4,256,256]{2,1,0:T(8,128)(2,1)} %k_in.1, bf16[4,256,256]{2,1,0:T(8,128)(2,1)} %v_in.1, bf16[256,2048]{1,0:T(8,128)(2,1)} %o_in.1, ...), custom_call_target="tpu_custom_call" | custom-call | tf_op jit(solution)/shard_map/layer/pallas_call | solution.py:695
  166.4 2.5 %hand_over.1 = (bf16[128,2048]{1,0:T(8,128)(2,1)}, bf16[128,2048]{1,0:T(8,128)(2,1)}, f32[64,768]{1,0:T(8,128)}, f32[64,768]{1,0:T(8,128)}, f32[64,768]{1,0:T(8,128)}) custom-call(bf16[128,2048]{1,0:T(8,128)(2,1)} %get-tuple-element.15.refs_0_, bf16[128,2048]{1,0:T(8,128)(2,1)} %get-tuple-element.16.refs_1_, f32[64,768]{1,0:T(8,128)} %get-tuple-element.17.refs_2_, ...), custom_call_target="tpu_custom_call" | custom-call | tf_op jit(solution)/shard_map/hand_over/pallas_call | solution.py:746

commit v7 on v6

--- a/solution.py
+++ b/solution.py
@@ -154,13 +154,14 @@
 
 def layer_kernel(
     q_in, k_in, v_in, o_in, gain_in, ids_in, weights_in, gate_in, up_in, down_in, grad_in,
-    layer_out, hidden_grad_out, gg_out, gu_out, gd_out,
+    layer_to, hidden_grad_to, gg_out, gu_out, gd_out,
     qs, kv, w, best, tot, acc, att, part_f, part_b, got,
     sel, sel_t, hidden_s, rows_s, grads_s, inv_s, inv_r, xr, cr, wg, wu, wd,
     act_g, act_u, act_b, act, act_back, xt, ct, grad, res, back, res_r, back_r,
     slots1_wide, slots1_slim, slots2_wide, slots2_slim, slot3_wide, slot3_slim,
     lsem, q_send, q_recv, w_send, w_recv, z_send, z_recv, g_send, g_recv, s_send, s_recv,
     a2a_local, a2a_send, a2a_recv, r_local, r_send, r_recv, rs_send, rs_recv,
+    layer_out, hidden_grad_out, out_sem,
 ):
     ctx, e, x, y, z = mesh_place()
     f32, bf = jnp.float32, jnp.bfloat16
@@ -617,6 +618,8 @@
         expert_sum = gates * jnp.dot(sel_t[...], returned[:, cols], preferred_element_type=f32)
         layer_out[:, cols] = (hidden_s[:, cols].astype(f32) + expert_sum).astype(bf)
 
+    layer_copy = pltpu.make_async_copy(layer_out, layer_to, out_sem.at[0])
+    layer_copy.start()
     arrive(back_x)
     returned = back_r[...].reshape(SLOTS, DM)
     shared = jnp.zeros((TOK, 1), f32)
@@ -636,6 +639,8 @@
             grad_in[:, cols].astype(f32) + inv_rms * (part_f[:, cols] - unit * shared)
         ).astype(bf)
 
+    hidden_copy = pltpu.make_async_copy(hidden_grad_out, hidden_grad_to, out_sem.at[1])
+    hidden_copy.start()
     for (first, width), (_, _, last, slot3) in zip(CHAINS, chains):
         cols = slice(first, first + width)
         last.wait_recv()
@@ -653,6 +658,8 @@
         else:
             gd_out[:, 256:768] = part_f[0:64, 640:1152]
 
+    layer_copy.wait()
+    hidden_copy.wait()
     for half in halves:
         half.wait_send()
     z_copy.wait_send()
@@ -696,7 +703,7 @@
         layer_kernel,
         out_shape=(rows, rows, shard, shard, shard),
         in_specs=[anywhere] * 4 + [vmem] * 3 + [anywhere] * 3 + [vmem],
-        out_specs=(vmem,) * 5,
+        out_specs=(anywhere,) * 2 + (vmem,) * 3,
         scratch_shapes=[
             pltpu.VMEM((4, 256, 256), bf),
             pltpu.VMEM((4, 4, 2, 2, 256, HEAD_SIZE), bf),
@@ -733,6 +740,7 @@
             dma(()), dma(()), dma((48,)), dma((48,)), dma((4,)), dma((4,)),
             dma((4,)), dma((4, 8)), dma((4, 8)), dma((4,)), dma((4, 8)), dma((4, 8)),
             dma((52,)), dma((52,)),
+            pltpu.VMEM((TOK, DM), bf), pltpu.VMEM((TOK, DM), bf), dma((2,)),
         ],
         compiler_params=pltpu.CompilerParams(
             collective_id=1, has_side_effects=True, vmem_limit_bytes=62 * 1024 * 1024

time: 169 us -> 167 us (0.988); the launches traced: 169 us -> 164 us
  Pallas kernels: 168 us -> 163 us
    pallas_call x1, Pallas kernels: 166 us -> 161 us  [on_device(): pl.pallas_call(layer_kernel, out_shape=(rows, rows, shard, shard, shard),...]
where the time goes in v7:
time: 167 us; the launch traced here: 164 us
  Pallas kernels  163 us (98%)
    pallas_call x1, Pallas kernels, on_device(): pl.pallas_call(layer_kernel, out_shape=(rows, rows, shard, shard, shard),...  161 us

profile of v7, /device:TPU:1, one launch (start us, length us, event | category | flops | bytes accessed | tf_op | source)
XLA Modules:
  0.0 163.9 jit_solution(8824136403662378532)
XLA Ops:
  0.6 160.7 %layer.1 = (bf16[128,2048]{1,0:T(8,128)(2,1)}, bf16[128,2048]{1,0:T(8,128)(2,1)}, f32[64,768]{1,0:T(8,128)}, f32[64,768]{1,0:T(8,128)}, f32[64,768]{1,0:T(8,128)}) custom-call(bf16[4,256,256]{2,1,0:T(8,128)(2,1)} %q_in.1, bf16[4,256,256]{2,1,0:T(8,128)(2,1)} %k_in.1, bf16[4,256,256]{2,1,0:T(8,128)(2,1)} %v_in.1, bf16[256,2048]{1,0:T(8,128)(2,1)} %o_in.1, ...), custom_call_target="tpu_custom_call" | custom-call | tf_op jit(solution)/shard_map/layer/pallas_call | solution.py:702
  161.3 2.5 %hand_over.1 = (bf16[128,2048]{1,0:T(8,128)(2,1)}, bf16[128,2048]{1,0:T(8,128)(2,1)}, f32[64,768]{1,0:T(8,128)}, f32[64,768]{1,0:T(8,128)}, f32[64,768]{1,0:T(8,128)}) custom-call(bf16[128,2048]{1,0:T(8,128)(2,1)} %get-tuple-element.15.refs_0_, bf16[128,2048]{1,0:T(8,128)(2,1)} %get-tuple-element.16.refs_1_, f32[64,768]{1,0:T(8,128)} %get-tuple-element.17.refs_2_, ...), custom_call_target="tpu_custom_call" | custom-call | tf_op jit(solution)/shard_map/hand_over/pallas_call | solution.py:754
